TPU v7x, 256 devices: a whole 4x4x8 slice. The times are simulated.
256 devices in a mesh: beam: 8 (over y, core), chan: 32 (over z, x).
Axes of the slice: x: 4, y: 4, z: 8, core: 2. Of those that a mesh axis runs over, the one named last changes fastest.
Arguments:
- observed: float32 [2, 1024, 4096], P(None, 'chan', 'beam'), parts along dimension 2, may hold values from -40 to 40
- window: float32 [4, 1024], replicated, may hold values from -1.5 to 1.5
- decays: float32 [1024, 4096], P('chan', 'beam'), parts along dimension 1, may hold values from 0.3 to 1
Outputs:
- solution: float32 [2, 4096, 1024], P(None, ('beam', 'chan')), parts along dimension 1
- residual: float32 [2, 4096, 1024], P(None, ('beam', 'chan')), parts along dimension 1
There are 8 independent parts, one for each index of `beam`. A program takes and returns all parts, laid end to end along the dimension named above; an argument that names none is the same for every part. Nothing has to cross between parts.
All inputs are finite; a program needn't handle non-finite values.
Results may differ from a plain program's by a relative error of at most 0.0003.
Values sent between devices are 32-bit elements; how exact they have to be, the bound alone decides.
A program may use at most 64 MiB of HBM per device.

v0:
```python
import math

import jax
import jax.numpy as jnp
from jax import lax
from jax.sharding import PartitionSpec as P

ITERS = 2


ridge = 0.5


def from_behind(value, axis, steps):
    count = lax.axis_size(axis)
    initial, last = (max(0, -steps), min(count, count - steps))
    return lax.ppermute(value, axis, [(source, source + steps) for source in range(initial, last)])


def running(decay, data):

    def combine(left, right):
        return (left[0] * right[0], right[0] * left[1] + right[1])

    return lax.associative_scan(combine, (decay, data), axis=2)


def whiten(data, decay, after, forward_fix, backward_fix):
    gain = 1.0 - decay
    prod_fwd, smooth = running(decay, gain * data)
    entering = forward_fix(prod_fwd[:, :, -1], smooth[:, :, -1])
    smooth = smooth + prod_fwd * entering[:, :, None]
    first = data + 2.0 * smooth
    prod_bwd, back = running(jnp.flip(after, 2), jnp.flip(first, 2))
    prod_bwd = jnp.flip(prod_bwd, 2)
    back = jnp.flip(back, 2)
    arriving = backward_fix(prod_bwd[:, :, 0], back[:, :, 0])
    back = back + prod_bwd * arriving[:, :, None]
    return first + 2.0 * gain * back


def no_fix(product, last):
    return jnp.zeros_like(last)


def body(observed, window, decays):
    count = window.shape[1]
    lag = window.shape[0] - 1
    hi = lax.Precision.HIGHEST
    index = lax.iota(jnp.int32, count)
    angle = (index[:, None] * index[None, :] % count).astype(jnp.float32) * (2.0 * math.pi / count)
    factor = 1.0 / math.sqrt(count)
    cosine = jnp.cos(angle) * factor
    sine = jnp.sin(angle) * factor

    def synthesise(spec):
        real = jnp.einsum("kn,kf->fn", cosine, spec[0], precision=hi) - jnp.einsum(
            "kn,kf->fn", sine, spec[1], precision=hi
        )
        imag = jnp.einsum("kn,kf->fn", cosine, spec[1], precision=hi) + jnp.einsum(
            "kn,kf->fn", sine, spec[0], precision=hi
        )
        wave = jnp.stack([real, imag])
        length = wave.shape[1]
        following = from_behind(wave[:, :lag, :], "chan", -1)
        extended = jnp.concatenate([wave, following], axis=1)
        result = window[0] * wave
        for tap in range(1, lag + 1):
            result = result + window[tap] * extended[:, tap : tap + length, :]
        return result

    decay = decays[None]
    after = jnp.concatenate([decay[:, :, 1:], jnp.zeros_like(decay[:, :, :1])], axis=2)

    def to_frames(spec):
        return lax.all_to_all(spec, "chan", split_axis=2, concat_axis=1, tiled=True)

    rhs = synthesise(to_frames(whiten(observed, decay, after, no_fix, no_fix)))

    def inner(left, right):
        return lax.psum(jnp.sum(left * right), "chan")

    solution = jnp.zeros_like(rhs)
    residual = rhs
    direction = rhs
    norm_now = inner(residual, residual)
    for step in range(ITERS):
        analyse_length = direction.shape[1]
        before = from_behind(direction[:, analyse_length - lag :, :], "chan", 1)
        analyse_extended = jnp.concatenate([before, direction], axis=1)
        mixed = window[0] * direction
        for analyse_tap in range(1, lag + 1):
            mixed = (
                mixed
                + window[analyse_tap]
                * analyse_extended[:, lag - analyse_tap : lag - analyse_tap + analyse_length, :]
            )
        analyse_real = jnp.einsum("kn,fn->kf", cosine, mixed[0], precision=hi) + jnp.einsum(
            "kn,fn->kf", sine, mixed[1], precision=hi
        )
        analyse_imag = jnp.einsum("kn,fn->kf", cosine, mixed[1], precision=hi) - jnp.einsum(
            "kn,fn->kf", sine, mixed[0], precision=hi
        )
        local = lax.all_to_all(
            jnp.stack([analyse_real, analyse_imag]), "chan", split_axis=1, concat_axis=2, tiled=True
        )
        image = (
            synthesise(to_frames(whiten(local, decay, after, no_fix, no_fix))) + ridge * direction
        )
        alpha = norm_now / inner(direction, image)
        solution = solution + alpha * direction
        residual = residual - alpha * image
        norm_next = inner(residual, residual)
        direction = residual + norm_next / norm_now * direction
        norm_now = norm_next
    return (solution, residual)


def solution(mesh):
    return jax.shard_map(
        body,
        mesh=mesh,
        in_specs=(P(None, "chan", "beam"), P(), P("chan", "beam")),
        out_specs=(P(None, ("beam", "chan"), None), P(None, ("beam", "chan"), None)),
        check_vma=False,
    )
```

profile of v0, /device:TPU:8, one launch (start us, length us, event | category | flops | bytes accessed | tf_op | source)
XLA Modules:
  0.0 780.3 jit_solution(17548902456327951890)
XLA Ops:
  27.8 22.0 %all_to_all.81 = f32[32,1,1024]{2,1,0:T(1,128)S(1)} all-to-all(f32[32,1,1024]{2,1,0:T(1,128)S(1)} %reshape.36), channel_id=1, replica_groups=mesh['beam'=8,'chan'=32] {'chan'}, dimensions={0} | all-to-all | bytes 262144 | tf_op jit(solution)/shard_map/all_to_all | solution.py:76
  52.1 17.7 %fusion.15 = f32[16,1024]{1,0:T(8,128)S(1)} fusion(f32[1024,16]{0,1:T(8,128)S(1)} %squeeze.40), kind=kOutput, calls=%fused_computation.20 | convolution fusion | flops 217055232 | bytes 131072 | tf_op jit(solution)/shard_map/kn,kf->fn/dot_general | solution.py:57
  70.1 17.7 %fusion.14 = f32[16,1024]{1,0:T(8,128)S(1)} fusion(f32[1024,16]{0,1:T(8,128)S(1)} %squeeze.41), kind=kOutput, calls=%fused_computation.19 | convolution fusion | flops 217055232 | bytes 131072 | tf_op jit(solution)/shard_map/kn,kf->fn/dot_general | solution.py:60
  87.8 18.0 %fusion.27 = f32[1,16,1024]{2,1,0:T(8,128)S(1)} fusion(f32[16,1024]{1,0:T(8,128)S(1)} %fusion.15, f32[1024,16]{0,1:T(8,128)S(1)} %squeeze.41), kind=kOutput, calls=%fused_computation.32 | convolution fusion | flops 217071616 | bytes 196608 | tf_op jit(solution)/shard_map/kn,kf->fn/dot_general | solution.py:57
  105.8 17.8 %fusion.29 = f32[1,16,1024]{2,1,0:T(8,128)S(1)} fusion(f32[16,1024]{1,0:T(8,128)S(1)} %fusion.14, f32[1024,16]{0,1:T(8,128)S(1)} %squeeze.40), kind=kOutput, calls=%fused_computation.34 | convolution fusion | flops 217071616 | bytes 196608 | tf_op jit(solution)/shard_map/kn,kf->fn/dot_general | solution.py:60
  133.3 19.7 %fusion.12 = f32[1024,16]{0,1:T(8,128)S(1)} fusion(f32[2,16,1024]{2,1,0:T(8,128)S(1)} %fusion.76), kind=kOutput, calls=%fused_computation.17 | convolution fusion | flops 217055232 | bytes 131072 | tf_op jit(solution)/shard_map/kn,fn->kf/dot_general | solution.py:101
  153.0 19.5 %fusion.13 = f32[1024,16]{0,1:T(8,128)S(1)} fusion(f32[2,16,1024]{2,1,0:T(8,128)S(1)} %fusion.76), kind=kOutput, calls=%fused_computation.18 | convolution fusion | flops 217055232 | bytes 131072 | tf_op jit(solution)/shard_map/kn,fn->kf/dot_general | solution.py:98
  172.5 20.1 %fusion.33 = f32[1,1024,16]{1,2,0:T(8,128)S(1)} fusion(f32[1024,16]{0,1:T(8,128)S(1)} %fusion.12, f32[2,16,1024]{2,1,0:T(8,128)S(1)} %fusion.76), kind=kOutput, calls=%fused_computation.38 | convolution fusion | flops 217071616 | bytes 196608 | tf_op jit(solution)/shard_map/kn,fn->kf/dot_general | solution.py:101
  192.6 19.7 %fusion.31 = f32[1,1024,16]{1,2,0:T(8,128)S(1)} fusion(f32[1024,16]{0,1:T(8,128)S(1)} %fusion.13, f32[2,16,1024]{2,1,0:T(8,128)S(1)} %fusion.76), kind=kOutput, calls=%fused_computation.36 | convolution fusion | flops 217071616 | bytes 196608 | tf_op jit(solution)/shard_map/kn,fn->kf/dot_general | solution.py:98
  214.3 19.9 %all_to_all.82 = f32[32,1,1024]{2,1,0:T(1,128)S(1)} all-to-all(f32[32,1,1024]{2,1,0:T(1,128)S(1)} %reshape.38), channel_id=1, replica_groups=mesh['beam'=8,'chan'=32] {'chan'}, dimensions={0} | all-to-all | bytes 262144 | tf_op jit(solution)/shard_map/all_to_all | solution.py:104
  266.4 17.7 %fusion.10 = f32[16,1024]{1,0:T(8,128)S(1)} fusion(f32[1024,16]{0,1:T(8,128)S(1)} %squeeze.45), kind=kOutput, calls=%fused_computation.15 | convolution fusion | flops 217055232 | bytes 131072 | tf_op jit(solution)/shard_map/kn,kf->fn/dot_general | solution.py:60
  302.0 18.2 %fusion.37 = f32[1,16,1024]{2,1,0:T(8,128)S(1)} fusion(f32[16,1024]{1,0:T(8,128)S(1)} %fusion.10, f32[1024,16]{0,1:T(8,128)S(1)} %squeeze.44), kind=kOutput, calls=%fused_computation.42 | convolution fusion | flops 217071616 | bytes 196608 | tf_op jit(solution)/shard_map/kn,kf->fn/dot_general | solution.py:60
  320.2 17.8 %fusion.35 = f32[1,16,1024]{2,1,0:T(8,128)S(1)} fusion(f32[16,1024]{1,0:T(8,128)S(1)} %fusion.11, f32[1024,16]{0,1:T(8,128)S(1)} %squeeze.45), kind=kOutput, calls=%fused_computation.40 | convolution fusion | flops 217071616 | bytes 196608 | tf_op jit(solution)/shard_map/kn,kf->fn/dot_general | solution.py:57
  344.7 70.5 %all-reduce.146 = (f32[]{:T(128)}, f32[]{:T(128)}) all-reduce(f32[]{:T(128)} %get-tuple-element.3, f32[]{:T(128)} %get-tuple-element.2), channel_id=1, replica_groups=mesh['beam'=8,'chan'=32] {'chan'}, use_global_device_ids=true, to_apply=%region_1.2 | all-reduce | flops 2 | bytes 16 | tf_op jit(solution)/shard_map/psum | solution.py:81
  417.2 72.1 %psum.30 = f32[]{:T(128)} all-reduce(f32[]{:T(128)} %multiply_reduce_fusion.1), channel_id=1, replica_groups=mesh['beam'=8,'chan'=32] {'chan'}, use_global_device_ids=true, to_apply=%region_5.6 | all-reduce | flops 1 | bytes 8 | tf_op jit(solution)/shard_map/psum | solution.py:81
  494.5 19.7 %fusion.8 = f32[1024,16]{0,1:T(8,128)S(1)} fusion(f32[2,16,1024]{2,1,0:T(8,128)S(1)} %fusion.69), kind=kOutput, calls=%fused_computation.13 | convolution fusion | flops 217055232 | bytes 131072 | tf_op jit(solution)/shard_map/kn,fn->kf/dot_general | solution.py:101
  514.2 19.5 %fusion.9 = f32[1024,16]{0,1:T(8,128)S(1)} fusion(f32[2,16,1024]{2,1,0:T(8,128)S(1)} %fusion.69), kind=kOutput, calls=%fused_computation.14 | convolution fusion | flops 217055232 | bytes 131072 | tf_op jit(solution)/shard_map/kn,fn->kf/dot_general | solution.py:98
  533.7 19.9 %fusion.41 = f32[1,1024,16]{1,2,0:T(8,128)S(1)} fusion(f32[1024,16]{0,1:T(8,128)S(1)} %fusion.8, f32[2,16,1024]{2,1,0:T(8,128)S(1)} %fusion.69), kind=kOutput, calls=%fused_computation.46 | convolution fusion | flops 217071616 | bytes 196608 | tf_op jit(solution)/shard_map/kn,fn->kf/dot_general | solution.py:101
  553.6 19.7 %fusion.39 = f32[1,1024,16]{1,2,0:T(8,128)S(1)} fusion(f32[1024,16]{0,1:T(8,128)S(1)} %fusion.9, f32[2,16,1024]{2,1,0:T(8,128)S(1)} %fusion.69), kind=kOutput, calls=%fused_computation.44 | convolution fusion | flops 217071616 | bytes 196608 | tf_op jit(solution)/shard_map/kn,fn->kf/dot_general | solution.py:98
  575.3 23.5 %all_to_all.84 = f32[32,1,1024]{2,1,0:T(1,128)S(1)} all-to-all(f32[32,1,1024]{2,1,0:T(1,128)S(1)} %reshape.42), channel_id=1, replica_groups=mesh['beam'=8,'chan'=32] {'chan'}, dimensions={0} | all-to-all | bytes 262144 | tf_op jit(solution)/shard_map/all_to_all | solution.py:104
  629.3 17.7 %fusion.6 = f32[16,1024]{1,0:T(8,128)S(1)} fusion(f32[1024,16]{0,1:T(8,128)S(1)} %squeeze.49), kind=kOutput, calls=%fused_computation.11 | convolution fusion | flops 217055232 | bytes 131072 | tf_op jit(solution)/shard_map/kn,kf->fn/dot_general | solution.py:60
  664.9 18.0 %fusion.45 = f32[1,16,1024]{2,1,0:T(8,128)S(1)} fusion(f32[16,1024]{1,0:T(8,128)S(1)} %fusion.6, f32[1024,16]{0,1:T(8,128)S(1)} %squeeze.48), kind=kOutput, calls=%fused_computation.50 | convolution fusion | flops 217071616 | bytes 196608 | tf_op jit(solution)/shard_map/kn,kf->fn/dot_general | solution.py:60
  683.0 17.8 %fusion.43 = f32[1,16,1024]{2,1,0:T(8,128)S(1)} fusion(f32[16,1024]{1,0:T(8,128)S(1)} %fusion.7, f32[1024,16]{0,1:T(8,128)S(1)} %squeeze.49), kind=kOutput, calls=%fused_computation.48 | convolution fusion | flops 217071616 | bytes 196608 | tf_op jit(solution)/shard_map/kn,kf->fn/dot_general | solution.py:57
  707.5 70.4 %psum.31 = f32[]{:T(128)} all-reduce(f32[]{:T(128)} %get-tuple-element.6), channel_id=1, replica_groups=mesh['beam'=8,'chan'=32] {'chan'}, use_global_device_ids=true, to_apply=%region_7.8 | all-reduce | flops 1 | bytes 8 | tf_op jit(solution)/shard_map/psum | solution.py:81
  (1051 shorter events, 155.0 us)
Async XLA Ops:
  123.6 29.4 %copy-start.9 = (f32[1,16,1024]{2,1,0:T(8,128)}, f32[1,16,1024]{2,1,0:T(8,128)S(1)}, u32[]{:S(2)}) copy-start(f32[1,16,1024]{2,1,0:T(8,128)S(1)} %fusion.29) | copy-start | bytes 196612
  123.6 5.8 collective-permute-start
  124.9 28.1 %copy-start.55 = (f32[1,1024]{1,0:T(1,128)}, f32[1,1024]{1,0:T(1,128)S(1)}, u32[]{:S(2)}) copy-start(f32[1,1024]{1,0:T(1,128)S(1)} %get-tuple-element.19) | copy-start | bytes 12292
  124.9 28.1 %copy-start.58 = (f32[1,1024]{1,0:T(1,128)}, f32[1,1024]{1,0:T(1,128)S(1)}, u32[]{:S(2)}) copy-start(f32[1,1024]{1,0:T(1,128)S(1)} %get-tuple-element.20) | copy-start | bytes 12292
  124.9 28.1 %copy-start.61 = (f32[1,1024]{1,0:T(1,128)}, f32[1,1024]{1,0:T(1,128)S(1)}, u32[]{:S(2)}) copy-start(f32[1,1024]{1,0:T(1,128)S(1)} %get-tuple-element.21) | copy-start | bytes 12292
  124.9 28.1 %copy-start.64 = (f32[1,1024]{1,0:T(1,128)}, f32[1,1024]{1,0:T(1,128)S(1)}, u32[]{:S(2)}) copy-start(f32[1,1024]{1,0:T(1,128)S(1)} %get-tuple-element.22) | copy-start | bytes 12292
  129.5 3.7 collective-permute-start.1
  320.2 23.7 %copy-start.10 = (f32[1,16,1024]{2,1,0:T(8,128)S(1)}, f32[1,16,1024]{2,1,0:T(8,128)}, u32[]{:S(2)}) copy-start(f32[1,16,1024]{2,1,0:T(8,128)} %copy-done.9) | copy-start | bytes 196612
  320.2 23.7 %copy-start.56 = (f32[1,1024]{1,0:T(1,128)S(1)}, f32[1,1024]{1,0:T(1,128)}, u32[]{:S(2)}) copy-start(f32[1,1024]{1,0:T(1,128)} %copy-done.55) | copy-start | bytes 12292
  320.2 23.7 %copy-start.59 = (f32[1,1024]{1,0:T(1,128)S(1)}, f32[1,1024]{1,0:T(1,128)}, u32[]{:S(2)}) copy-start(f32[1,1024]{1,0:T(1,128)} %copy-done.58) | copy-start | bytes 12292
  320.2 23.7 %copy-start.62 = (f32[1,1024]{1,0:T(1,128)S(1)}, f32[1,1024]{1,0:T(1,128)}, u32[]{:S(2)}) copy-start(f32[1,1024]{1,0:T(1,128)} %copy-done.61) | copy-start | bytes 12292
  320.2 23.7 %copy-start.65 = (f32[1,1024]{1,0:T(1,128)S(1)}, f32[1,1024]{1,0:T(1,128)}, u32[]{:S(2)}) copy-start(f32[1,1024]{1,0:T(1,128)} %copy-done.64) | copy-start | bytes 12292
  338.0 5.8 collective-permute-start.2
  344.7 169.5 %copy-start.14 = (f32[2,16,1024]{2,1,0:T(8,128)}, f32[2,16,1024]{2,1,0:T(8,128)S(1)}, u32[]{:S(2)}) copy-start(f32[2,16,1024]{2,1,0:T(8,128)S(1)} %get-tuple-element.8) | copy-start | bytes 393220
  490.7 23.5 %copy-start.12 = (f32[2,16,1024]{2,1,0:T(8,128)}, f32[2,16,1024]{2,1,0:T(8,128)S(1)}, u32[]{:S(2)}) copy-start(f32[2,16,1024]{2,1,0:T(8,128)S(1)} %multiply_add_fusion.13) | copy-start | bytes 393220
  490.8 3.7 collective-permute-start.3
  682.9 23.8 %copy-start.13 = (f32[2,16,1024]{2,1,0:T(8,128)S(1)}, f32[2,16,1024]{2,1,0:T(8,128)}, u32[]{:S(2)}) copy-start(f32[2,16,1024]{2,1,0:T(8,128)} %copy-done.12) | copy-start | bytes 393220
  683.0 23.8 %copy-start.57 = (f32[1,1024]{1,0:T(1,128)S(1)}, f32[1,1024]{1,0:T(1,128)}, u32[]{:S(2)}) copy-start(f32[1,1024]{1,0:T(1,128)} %copy-done.55) | copy-start | bytes 12292
  683.0 23.8 %copy-start.60 = (f32[1,1024]{1,0:T(1,128)S(1)}, f32[1,1024]{1,0:T(1,128)}, u32[]{:S(2)}) copy-start(f32[1,1024]{1,0:T(1,128)} %copy-done.58) | copy-start | bytes 12292
  683.0 23.8 %copy-start.63 = (f32[1,1024]{1,0:T(1,128)S(1)}, f32[1,1024]{1,0:T(1,128)}, u32[]{:S(2)}) copy-start(f32[1,1024]{1,0:T(1,128)} %copy-done.61) | copy-start | bytes 12292
  683.0 23.8 %copy-start.66 = (f32[1,1024]{1,0:T(1,128)S(1)}, f32[1,1024]{1,0:T(1,128)}, u32[]{:S(2)}) copy-start(f32[1,1024]{1,0:T(1,128)} %copy-done.64) | copy-start | bytes 12292
  700.8 78.4 %copy-start.11 = (f32[1,16,1024]{2,1,0:T(8,128)S(1)}, f32[1,16,1024]{2,1,0:T(8,128)}, u32[]{:S(2)}) copy-start(f32[1,16,1024]{2,1,0:T(8,128)} %copy-done.9) | copy-start | bytes 196612
  700.8 78.4 %copy-start.15 = (f32[2,16,1024]{2,1,0:T(8,128)S(1)}, f32[2,16,1024]{2,1,0:T(8,128)}, u32[]{:S(2)}) copy-start(f32[2,16,1024]{2,1,0:T(8,128)} %copy-done.14) | copy-start | bytes 393220
  700.8 5.9 collective-permute-start.4
  (134 other events, 395.8 us)
where the time goes:
time: 788 us; the launch traced here: 780 us
  matrix products  371 us (47%)
  blocking collectives  306 us (39%)
  local copies, waits for them, and re-layouts  48.6 us (6%)
  other arithmetic  18.2 us (2%)
  waiting for transfers between devices  16.6 us (2%)
  between operations  10.9 us (1%)
  starting transfers between devices  8.21 us (1%)
    psum x3, blocking collectives, inner(): return lax.psum(jnp.sum(left * right), 'chan')  213 us
    dot_general x3, matrix products, synthesise(): jnp.einsum('kn,kf->fn', sine, spec[0], precision=hi)  54 us
    dot_general x3, matrix products, synthesise(): jnp.einsum('kn,kf->fn', sine, spec[1], precision=hi)  53.5 us
    dot_general x3, matrix products, synthesise(): jnp.einsum('kn,kf->fn', cosine, spec[1], precision=hi)  53.1 us
    dot_general x3, matrix products, synthesise(): jnp.einsum('kn,kf->fn', cosine, spec[0], precision=hi)  53.1 us
    all_to_all x3, blocking collectives, to_frames(): return lax.all_to_all(spec, 'chan', split_axis=2, concat_axis=1, tiled=True)  50 us
    all_to_all x2, blocking collectives, body(): lax.all_to_all(jnp.stack([analyse_real, analyse_imag]), 'chan', split_axi...  43.4 us
    dot_general x2, matrix products, body(): jnp.einsum('kn,fn->kf', sine, mixed[0], precision=hi)  39.9 us
  transfers between devices with their start and end apart: 5, of which 5 were waited for; matrix products, arithmetic and copies ran while one was open for 0% of the time, Pallas kernels for 0%

commit v1 on v0

v1 whole, which is shorter than its diff:
```python
import functools
import math

import jax
import jax.numpy as jnp
import ml_dtypes
import numpy as np
from jax import lax
from jax.experimental import pallas as pl
from jax.experimental.pallas import tpu as pltpu
from jax.sharding import PartitionSpec as P

MESH = pl.DeviceIdType.MESH
F32 = jnp.float32
BF16 = jnp.bfloat16
GROUP = 32
NX = 4
NZ = 8
RIDGE = 0.5
FLIP = (0, 4, 2, 6, 1, 5, 3, 7)


def tables():
    lane = np.arange(128)
    k2 = 4 * (lane % 32) + lane // 32
    n2 = np.arange(128)
    angle = 2.0 * np.pi * ((k2[:, None] * n2[None, :]) % 128) / 128.0
    cos, sin = np.cos(angle) / 32.0, np.sin(angle) / 32.0
    inverse = np.block([[cos, sin], [-sin, cos]])

    def split(matrix):
        high = matrix.astype(ml_dtypes.bfloat16)
        low = (matrix - high.astype(np.float64)).astype(ml_dtypes.bfloat16)
        return np.concatenate([high, high, low], axis=0)

    mats = np.stack([split(inverse), split(inverse.T)])
    turn = 2.0 * np.pi * np.array(FLIP)[:, None] * n2[None, :] / 1024.0
    eighth = 2.0 * np.pi * np.maximum(np.arange(8) - 4, 0) / 8.0
    eighth = np.broadcast_to(eighth[:, None], (8, 128))
    tabs = np.stack([np.cos(turn), np.sin(turn), np.cos(eighth), np.sin(eighth)])
    return mats, tabs.astype(np.float32)


def kernel(
    obs_hbm, win_hbm, dec_hbm, mats_hbm, tabs_hbm, sol_ref, res_ref,
    obs_v, win_v, dec_v, mats_v, tabs_v, stage, got,
    spec, dec, e0_s, carry_x, carry_z, xb, zb, cx, cz, sb,
    in_sem, own_sem, a_send, a_recv, xc_send, xc_recv, zc_send, zc_recv,
    x_send, x_recv, z_send, z_recv, s_send, s_recv,
):
    me = lax.axis_index("chan")
    mz = me // NX
    mx = lax.rem(me, NX)
    inputs = []
    for t, (src, dst) in enumerate(
        ((obs_hbm, obs_v), (dec_hbm, dec_v), (win_hbm, win_v), (mats_hbm, mats_v), (tabs_hbm, tabs_v))
    ):
        copy = pltpu.make_async_copy(src, dst, in_sem.at[t])
        copy.start()
        inputs.append(copy)
    barrier = pltpu.get_barrier_semaphore()
    for t in range(1, GROUP):
        pl.semaphore_signal(
            barrier, inc=1, device_id={"chan": lax.rem(me + t, GROUP)}, device_id_type=MESH
        )
    inputs[0].wait()
    inputs[1].wait()

    frames = 512
    lane = lax.broadcasted_iota(jnp.int32, (32, frames), 1)
    row = lax.rem(lax.broadcasted_iota(jnp.int32, (32, frames), 0), 8)

    def shift(value, steps):
        return pltpu.roll(value, steps % frames, axis=value.ndim - 1)

    a = dec_v[...]
    gain = 1.0 - a
    data = [obs_v[0], obs_v[1]]
    prod = jnp.where(lane == 0, 0.0, a)
    run = [gain * d for d in data]
    step = 1
    while step < frames:
        run = [r + prod * shift(r, step) for r in run]
        prod = prod * shift(prod, step)
        step *= 2
    first = [d + 2.0 * r for d, r in zip(data, run)]
    prod = jnp.where(lane == frames - 1, 0.0, shift(a, -1))
    run = first
    step = 1
    while step < frames:
        run = [r + prod * shift(r, -step) for r in run]
        prod = prod * shift(prod, -step)
        step *= 2
    white = [f + 2.0 * gain * r for f, r in zip(first, run)]

    up = (row == 1) | (row == 3)
    down = (row == 4) | (row == 6)

    def flipped(value):
        return jnp.where(
            up,
            pltpu.roll(value, 29, axis=0),
            jnp.where(down, pltpu.roll(value, 3, axis=0), value),
        )

    def moved(value, offset):
        moved_value = shift(value, -offset)
        inside = (lane + offset >= 0) & (lane + offset < frames)
        return jnp.where(inside, moved_value, 0.0)

    white = [flipped(w) for w in white]
    af = flipped(a)
    packed = jnp.concatenate(
        [moved(white[0], -6), moved(white[1], -6), moved(white[0], 10), moved(white[1], 10)], axis=0
    )
    stage[:, 0:16, :] = packed.T.reshape(GROUP, 16, 128)
    packed = jnp.concatenate([moved(af, 8 * t - 6) for t in range(4)], axis=0)
    stage[:, 16:24, :] = packed.T.reshape(GROUP, 16, 128)[:, :8]

    pl.semaphore_wait(barrier, GROUP - 1)

    spreads = []
    for t in range(1, GROUP):
        to = lax.rem(me + t, GROUP)
        copy = pltpu.make_async_remote_copy(
            src_ref=stage.at[to], dst_ref=got.at[:, me, :], send_sem=a_send.at[t], recv_sem=a_recv.at[t],
            device_id={"chan": to}, device_id_type=MESH,
        )
        copy.start()
        spreads.append(copy)
    own = pltpu.make_async_copy(stage.at[me], got.at[:, me, :], own_sem)
    own.start()
    for copy in inputs[2:]:
        copy.wait()

    win = [
        jnp.concatenate([win_v[p : p + 1, n * 128 : (n + 1) * 128] for n in range(8)], axis=0)
        for p in range(4)
    ]

    def butterfly(value, distance):
        index = lax.broadcasted_iota(jnp.int32, value.shape, 1)
        high = (index & distance) != 0
        if distance == 4:
            other = pltpu.roll(value, 4, axis=1)
        else:
            other = jnp.where(
                high, pltpu.roll(value, distance, axis=1), pltpu.roll(value, 8 - distance, axis=1)
            )
        return jnp.where(high, other - value, other + value)

    def quarter(re, im, sign):
        index = lax.broadcasted_iota(jnp.int32, re.shape, 1)
        turned = (index & 3) == 3
        return jnp.where(turned, -sign * im, re), jnp.where(turned, sign * re, im)

    def times(re, im, c, s):
        return re * c - im * s, re * s + im * c

    def product(re, im, which):
        count = re.shape[0]
        x = jnp.concatenate([re.reshape(count * 8, 128), im.reshape(count * 8, 128)], axis=1)
        high = x.astype(BF16)
        low = (x - high.astype(F32)).astype(BF16)
        y = jnp.dot(
            jnp.concatenate([high, low, high], axis=1), mats_v[which], preferred_element_type=F32
        )
        return y[:, :128].reshape(count, 8, 128), y[:, 128:].reshape(count, 8, 128)

    def to_wave(re, im):
        re, im = product(re, im, 0)
        re, im = times(re, im, tabs_v[0], tabs_v[1])
        re, im = butterfly(re, 1), butterfly(im, 1)
        re, im = quarter(re, im, 1.0)
        re, im = butterfly(re, 2), butterfly(im, 2)
        re, im = times(re, im, tabs_v[2], tabs_v[3])
        return butterfly(re, 4), butterfly(im, 4)

    def to_spec(re, im):
        re, im = butterfly(re, 4), butterfly(im, 4)
        re, im = times(re, im, tabs_v[2], -tabs_v[3])
        re, im = butterfly(re, 2), butterfly(im, 2)
        re, im = quarter(re, im, -1.0)
        re, im = butterfly(re, 1), butterfly(im, 1)
        re, im = times(re, im, tabs_v[0], -tabs_v[1])
        return product(re, im, 1)

    def gather_taps(u, count):
        out = win[0] * u[0:count]
        for p in range(1, 4):
            out = out + win[p] * u[p : p + count]
        return out

    def spread_taps(v, count):
        out = win[0] * v[3 : 3 + count]
        for p in range(1, 4):
            out = out + win[p] * v[3 - p : 3 - p + count]
        return out

    def keep(value, start, before, after):
        index = lax.broadcasted_iota(jnp.int32, value.shape, 0) + start
        out = value
        if before:
            out = jnp.where((index < 6) & (me == 0), 0.0, out)
        if after:
            out = jnp.where((index >= 22) & (me == GROUP - 1), 0.0, out)
        return out

    own.wait()
    for copy in spreads:
        copy.wait_recv()

    lane8 = lax.broadcasted_iota(jnp.int32, (8, 128), 1)
    low64 = lane8 < 64
    low32 = (lane8 & 32) == 0

    def exchange(v):
        y = [None] * 4
        for i in range(2):
            y[i] = jnp.where(low64, v[i], pltpu.roll(v[i + 2], 64, axis=1))
            y[i + 2] = jnp.where(low64, pltpu.roll(v[i], 64, axis=1), v[i + 2])
        z = [None] * 4
        for i in (0, 2):
            z[i] = jnp.where(low32, y[i], pltpu.roll(y[i + 1], 32, axis=1))
            z[i + 1] = jnp.where(low32, pltpu.roll(y[i], 96, axis=1), y[i + 1])
        return z

    for q in range(2):
        turned = got[16 + 4 * q : 20 + 4 * q].reshape(128, 128).T
        for part in range(4):
            base = part * 32
            out = exchange([turned[base + 8 * i : base + 8 * i + 8] for i in range(4)])
            for r in range(4):
                dec[8 * part + 4 * q + r] = out[r]

    def coefficients(start, count):
        stop = start + count
        p = dec[start]
        ps = [p]
        for g in range(start + 1, stop):
            p = dec[g] * p
            ps.append(p)
        b = dec[stop]
        h = ps[-1]
        bs, hs = [b], [h]
        for g in range(stop - 2, start - 1, -1):
            b = dec[g + 1] * b
            h = ps[g - start] + dec[g + 1] * h
            bs.append(b)
            hs.append(h)
        bs.reverse()
        hs.reverse()
        two_p = jnp.stack([2.0 * v for v in ps])
        gains = [2.0 * (1.0 - dec[g]) for g in range(start, stop)]
        left = jnp.stack([2.0 * x + 2.0 * y * z for x, y, z in zip(ps, gains, hs)])
        right = jnp.stack([y * z for y, z in zip(gains, bs)])
        return two_p, left, right, ps[15], bs[count - 16], 2.0 * hs[count - 16]

    two_p0, left0, right0, a0, b0, k0 = coefficients(3, 25)
    two_p1, left1, right1, a1, b1, k1 = coefficients(6, 19)
    for n, value in enumerate((a0, b0, k0, a1, b1, k1)):
        cx[mx, 8 * n : 8 * n + 8] = value

    def x_copies(src, dst, send, recv):
        out = []
        for t in range(1, NX):
            to = mz * NX + lax.rem(mx + t, NX)
            out.append(pltpu.make_async_remote_copy(
                src_ref=src, dst_ref=dst, send_sem=send.at[t], recv_sem=recv.at[t],
                device_id={"chan": to}, device_id_type=MESH,
            ))
        for copy in out:
            copy.start()
        return out

    def z_copies(src, dst, send, recv):
        out = []
        for t in range(1, NZ):
            to = lax.rem(mz + t, NZ) * NX + mx
            out.append(pltpu.make_async_remote_copy(
                src_ref=src, dst_ref=dst, send_sem=send.at[t], recv_sem=recv.at[t],
                device_id={"chan": to}, device_id_type=MESH,
            ))
        for copy in out:
            copy.start()
        return out

    sent = list(spreads)
    x_coefs = x_copies(cx.at[mx], cx.at[mx], xc_send, xc_recv)
    sent += x_coefs

    for q in range(4):
        turned = got[4 * q : 4 * q + 4].reshape(128, 128).T
        for half in range(2):
            for c in range(2):
                base = half * 64 + c * 32
                out = exchange([turned[base + 8 * i : base + 8 * i + 8] for i in range(4)])
                for r in range(4):
                    spec[c, 16 * half + 4 * q + r] = out[r]

    def local_whiten(re, im, start, count):
        stop = start + count
        x = [jnp.stack([re[g], im[g]]) for g in range(count)]
        s = (1.0 - dec[start]) * x[0]
        e = [x[0] + 2.0 * s]
        leaving_right = None
        for g in range(1, count):
            a = dec[start + g]
            s = a * s + (1.0 - a) * x[g]
            e.append(x[g] + 2.0 * s)
            if g == 15:
                leaving_right = s
        back = e[-1]
        w = [None] * count
        leaving_left = None
        w[-1] = e[-1] + 2.0 * (1.0 - dec[stop - 1]) * back
        for g in range(count - 2, -1, -1):
            back = e[g] + dec[start + g + 1] * back
            w[g] = e[g] + 2.0 * (1.0 - dec[start + g]) * back
            if g == count - 16:
                leaving_left = back
        return e, w, leaving_right, leaving_left

    def chain(carry, back, left, right, a, b, k):
        count = len(left)
        cs = [carry]
        for n in range(count):
            cs.append(a[n] * cs[n] + left[n])
        ds = [None] * count
        d = back
        for n in range(count - 1, -1, -1):
            ds[n] = d
            d = b[n] * d + (right[n] + k[n] * cs[n])
        return cs, ds, d

    def pair(ref, base):
        return jnp.stack([ref[base : base + 8], ref[base + 8 : base + 16]])

    zero = jnp.zeros((2, 8, 128), F32)

    def x_side(turn):
        c = [[cx[n, 24 * turn + 8 * m : 24 * turn + 8 * m + 8] for n in range(NX)] for m in range(3)]
        return c

    def group_coefficients(turn):
        a, b, k = x_side(turn)
        ga, gb, gk = a[0], b[0], k[0]
        for n in range(1, NX):
            gk = gb * k[n] * ga + gk
            gb = gb * b[n]
            ga = a[n] * ga
        cz[turn, mz, 0:8] = ga
        cz[turn, mz, 8:16] = gb
        cz[turn, mz, 16:24] = gk

    def carries(turn, right_going, left_going, rows):
        nrow = 32 + len(rows)
        xv = xb.at[turn, mx]
        xv[0:8] = right_going[0]
        xv[8:16] = right_going[1]
        xv[16:24] = left_going[0]
        xv[24:32] = left_going[1]
        for n, value in enumerate(rows):
            xv[32 + n : 33 + n] = value
        part = xb.at[turn, mx, pl.ds(0, nrow)]
        copies = x_copies(part, part, x_send.at[turn], x_recv.at[turn])
        sent.extend(copies)
        if turn == 0:
            for copy in x_coefs:
                copy.wait_recv()
            for which in range(2):
                group_coefficients(which)
            sent.extend(z_coefs_start(0))
        for copy in copies:
            copy.wait_recv()
        a, b, k = x_side(turn)
        left = [pair(xb.at[turn, n], 0) for n in range(NX)]
        right = [pair(xb.at[turn, n], 16) for n in range(NX)]
        cs, ds, out = chain(zero, zero, left, right, a, b, k)
        zv = zb.at[turn, mz]
        zv[0:8] = cs[NX][0]
        zv[8:16] = cs[NX][1]
        zv[16:24] = out[0]
        zv[24:32] = out[1]
        for n in range(len(rows)):
            total = xb[turn, 0, 32 + n : 33 + n]
            for m in range(1, NX):
                total = total + xb[turn, m, 32 + n : 33 + n]
            zv[32 + n : 33 + n] = total
        part = zb.at[turn, mz, pl.ds(0, nrow)]
        copies = z_copies(part, part, z_send.at[turn], z_recv.at[turn])
        sent.extend(copies)
        if turn == 0:
            sent.extend(z_coefs_start(1))
        for copy in z_coefs[turn]:
            copy.wait_recv()
        for copy in copies:
            copy.wait_recv()
        za, zbk, zk = [[cz[turn, n, 8 * m : 8 * m + 8] for n in range(NZ)] for m in range(3)]
        zleft = [pair(zb.at[turn, n], 0) for n in range(NZ)]
        zright = [pair(zb.at[turn, n], 16) for n in range(NZ)]
        zcs, zds, _ = chain(zero, zero, zleft, zright, za, zbk, zk)
        for n in range(NZ):
            carry_z[0, n] = zcs[n]
            carry_z[1, n] = zds[n]
        cs, ds, _ = chain(carry_z[0, mz], carry_z[1, mz], left, right, a, b, k)
        for n in range(NX):
            carry_x[0, n] = cs[n]
            carry_x[1, n] = ds[n]
        sums = []
        for n in range(len(rows)):
            total = zb[turn, 0, 32 + n : 33 + n]
            for m in range(1, NZ):
                total = total + zb[turn, m, 32 + n : 33 + n]
            sums.append(jnp.sum(total, axis=1, keepdims=True))
        return carry_x[0, mx], carry_x[1, mx], sums

    z_coefs = [None, None]

    def z_coefs_start(turn):
        z_coefs[turn] = z_copies(
            cz.at[turn, mz], cz.at[turn, mz], zc_send.at[turn], zc_recv.at[turn]
        )
        return z_coefs[turn]

    def corrected(w, left, right, c, d):
        re = jnp.stack([v[0] for v in w]) + left * c[0] + right * d[0]
        im = jnp.stack([v[1] for v in w]) + left * c[1] + right * d[1]
        return re, im

    def padded(re, im):
        fill = jnp.zeros((1, 8, 128), F32)
        return jnp.concatenate([re, fill]), jnp.concatenate([im, fill])

    def folded(value):
        return jnp.sum(jnp.sum(value, axis=0), axis=0, keepdims=True)

    u = to_wave(spec[0], spec[1])
    r0 = [keep(gather_taps(v, 29), 0, True, False) for v in u]
    x = to_spec(*[spread_taps(v, 26) for v in r0])
    x = [keep(v, 3, False, True) for v in x]
    e0, w0, going_right, going_left = local_whiten(x[0], x[1], 3, 25)
    c, d, _ = carries(0, going_right, going_left, [])
    for n in range(2):
        e0_s[n] = jnp.stack([v[n] for v in e0[3:19]]) + two_p0[3:19] * c[n]
    w = corrected(w0, left0, right0, c, d)

    u = to_wave(*padded(*w))
    q1 = [
        keep(gather_taps(v, 22) + RIDGE * r[3:25], 3, True, False) for v, r in zip(u, r0)
    ]
    mine_r0 = [v[6:22] for v in r0]
    mine_q1 = [v[3:19] for v in q1]
    rr_part = folded(mine_r0[0] * mine_r0[0] + mine_r0[1] * mine_r0[1])
    rq_part = folded(mine_r0[0] * mine_q1[0] + mine_r0[1] * mine_q1[1])
    x = to_spec(*padded(*[spread_taps(v, 19) for v in q1]))
    x = [keep(v, 6, False, True) for v in x]
    e1, w1, going_right, going_left = local_whiten(x[0], x[1], 6, 19)
    c, d, (rr, rq) = carries(1, going_right, going_left, [rr_part, rq_part])
    alpha = rr / rq

    r1 = [r - alpha * q for r, q in zip(mine_r0, mine_q1)]
    energy = []
    for n in range(2):
        e = e0_s[n] - alpha * (jnp.stack([v[n] for v in e1[:16]]) + two_p1[:16] * c[n])
        energy.append(e * e)
    new_part = folded(r1[0] * r1[0] + r1[1] * r1[1])
    energy_part = folded(energy[0] + energy[1])
    new_part = new_part + pltpu.roll(new_part, 64, axis=1)
    energy_part = energy_part + pltpu.roll(energy_part, 64, axis=1)
    low = lax.broadcasted_iota(jnp.int32, (1, 128), 1) < 64
    sb[me] = jnp.where(low, new_part, energy_part)
    lasts = []
    for t in range(1, GROUP):
        to = lax.rem(me + t, GROUP)
        copy = pltpu.make_async_remote_copy(
            src_ref=sb.at[me], dst_ref=sb.at[me], send_sem=s_send.at[t], recv_sem=s_recv.at[t],
            device_id={"chan": to}, device_id_type=MESH,
        )
        copy.start()
        lasts.append(copy)
    sent += lasts

    w = corrected(w1, left1, right1, c, d)
    u = to_wave(*padded(*w))
    q2 = [gather_taps(v, 16) + RIDGE * q for v, q in zip(u, mine_q1)]
    n1 = [q - alpha * p for q, p in zip(mine_q1, q2)]

    for copy in lasts:
        copy.wait_recv()
    total = sb[0]
    for n in range(1, GROUP):
        total = total + sb[n]
    new = jnp.sum(jnp.where(low, total, 0.0), axis=1, keepdims=True)
    energy = jnp.sum(jnp.where(low, 0.0, total), axis=1, keepdims=True)
    beta = new / rr
    alpha_next = new / (energy + RIDGE * new - beta * new / alpha)
    for n in range(2):
        direction = r1[n] + beta * mine_r0[n]
        image = n1[n] + beta * mine_q1[n]
        sol = alpha * mine_r0[n] + alpha_next * direction
        res = r1[n] - alpha_next * image
        sol_ref[n] = sol.reshape(16, 1024)
        res_ref[n] = res.reshape(16, 1024)
    for copy in sent:
        copy.wait_send()


def body(observed, window, decays):
    mats, tabs = tables()
    any_space = pl.BlockSpec(memory_space=pl.ANY)
    vmem = pl.BlockSpec(memory_space=pltpu.VMEM)
    dma = pltpu.SemaphoreType.DMA
    out = jax.ShapeDtypeStruct((2, 16, 1024), F32)
    return pl.pallas_call(
        kernel,
        out_shape=(out, out),
        in_specs=[any_space] * 5,
        out_specs=(vmem, vmem),
        scratch_shapes=[
            pltpu.VMEM((2, 32, 512), F32),
            pltpu.VMEM((4, 1024), F32),
            pltpu.VMEM((32, 512), F32),
            pltpu.VMEM((2, 768, 256), BF16),
            pltpu.VMEM((4, 8, 128), F32),
            pltpu.VMEM((GROUP, 24, 128), F32),
            pltpu.VMEM((24, GROUP, 128), F32),
            pltpu.VMEM((2, 32, 8, 128), F32),
            pltpu.VMEM((32, 8, 128), F32),
            pltpu.VMEM((2, 16, 8, 128), F32),
            pltpu.VMEM((2, NX, 2, 8, 128), F32),
            pltpu.VMEM((2, NZ, 2, 8, 128), F32),
            pltpu.VMEM((2, NX, 40, 128), F32),
            pltpu.VMEM((2, NZ, 40, 128), F32),
            pltpu.VMEM((NX, 48, 128), F32),
            pltpu.VMEM((2, NZ, 24, 128), F32),
            pltpu.VMEM((GROUP, 1, 128), F32),
            dma((5,)),
            dma,
            dma((GROUP,)), dma((GROUP,)),
            dma((NX,)), dma((NX,)),
            dma((2, NZ)), dma((2, NZ)),
            dma((2, NX)), dma((2, NX)),
            dma((2, NZ)), dma((2, NZ)),
            dma((GROUP,)), dma((GROUP,)),
        ],
        name="invert",
        compiler_params=pltpu.CompilerParams(
            collective_id=0, has_side_effects=True, vmem_limit_bytes=48 * 1024 * 1024
        ),
    )(observed, window, decays, jnp.asarray(mats), jnp.asarray(tabs))


def solution(mesh):
    return jax.shard_map(
        body,
        mesh=mesh,
        in_specs=(P(None, "chan", "beam"), P(), P("chan", "beam")),
        out_specs=(P(None, ("beam", "chan"), None), P(None, ("beam", "chan"), None)),
        check_vma=False,
    )
```

time: 788 us -> 58.8 us (0.07)
  matrix products: 371 us -> 0 us
  blocking collectives: 306 us -> 0 us
  Pallas kernels: 0 us -> 52.2 us
  local copies, waits for them, and re-layouts: 48.6 us -> 5.62 us
  other arithmetic: 18.2 us -> 0 us
  waiting for transfers between devices: 16.6 us -> 0 us
  between operations: 10.9 us -> 0.65 us
  starting transfers between devices: 8.21 us -> 0 us
    dot_general x20 -> x0, matrix products: 371 us -> none  [the longest x3 54 us: synthesise(): jnp.einsum('kn,kf->fn', sine, spec[0], precision=hi)]
    psum x3 -> x0, blocking collectives: 213 us -> none  [inner(): return lax.psum(jnp.sum(left * right), 'chan')]
    all_to_all x5 -> x0, blocking collectives: 93.4 us -> none  [the longest x3 50 us: to_frames(): return lax.all_to_all(spec, 'chan', split_axis=2, concat_axis=1, tiled=True)]
    pallas_call x0 -> x1, Pallas kernels: none -> 52.2 us  [body(): pl.pallas_call(kernel, out_shape=(out, out), in_specs=[any_space] * 5, ou...]
    slice x268 -> x0, local copies, waits for them, and re-layouts: 19.5 us -> none  [the longest x255 18.8 us: running(): return lax.associative_scan(combine, (decay, data), axis=2)]
    ppermute x5 -> x0, waiting for transfers between devices: 16.6 us -> none  [from_behind(): lax.ppermute(value, axis, [(source, source + steps) for source in range(i...]
    unnamed x316 -> x12, local copies, waits for them, and re-layouts: 18.3 us -> 5.62 us
    ppermute x5 -> x0, starting transfers between devices: 8.21 us -> none  [from_behind(): lax.ppermute(value, axis, [(source, source + steps) for source in range(i...]
  transfers between devices with their start and end apart: 5 -> 0, of which waited for: 5 -> 0; matrix products, arithmetic and copies ran while one was open for 0% -> 0% of each run, Pallas kernels for 0% -> 0%
where the time goes in v1:
time: 58.8 us; the launch traced here: 58.5 us
  Pallas kernels  52.2 us (89%)
  local copies, waits for them, and re-layouts  5.62 us (10%)
  between operations  0.65 us (1%)
    pallas_call x1, Pallas kernels, body(): pl.pallas_call(kernel, out_shape=(out, out), in_specs=[any_space] * 5, ou...  52.2 us
    unnamed x12, local copies, waits for them, and re-layouts  5.62 us

profile of v1, /device:TPU:8, one launch (start us, length us, event | category | flops | bytes accessed | tf_op | source)
XLA Modules:
  0.0 58.5 jit_solution(15076689045573475550)
XLA Ops:
  0.6 0.0 copy-start
  0.6 1.1 %copy-done = bf16[2,768,256]{2,1,0:T(8,128)(2,1)S(1)} copy-done((bf16[2,768,256]{2,1,0:T(8,128)(2,1)S(1)}, bf16[2,768,256]{2,1,0:T(8,128)(2,1)}, u32[]{:S(2)}) %copy-start) | copy-done | bytes 786456
  1.8 0.0 copy-start.1
  1.8 0.9 %copy-done.1 = f32[2,32,512]{2,1,0:T(8,128)S(1)} copy-done((f32[2,32,512]{2,1,0:T(8,128)S(1)}, f32[2,32,512]{2,1,0:T(8,128)}, u32[]{:S(2)}) %copy-start.1) | copy-done | bytes 131096
  2.7 0.0 copy-start.2
  2.7 0.8 %copy-done.2 = f32[32,512]{1,0:T(8,128)S(1)} copy-done((f32[32,512]{1,0:T(8,128)S(1)}, f32[32,512]{1,0:T(8,128)}, u32[]{:S(2)}) %copy-start.2) | copy-done | bytes 65560
  3.5 0.0 copy-start.3
  3.5 0.7 %copy-done.3 = f32[4,1024]{1,0:T(4,128)S(1)} copy-done((f32[4,1024]{1,0:T(4,128)S(1)}, f32[4,1024]{1,0:T(4,128)}, u32[]{:S(2)}) %copy-start.3) | copy-done | bytes 16408
  4.2 0.0 copy-start.4
  4.2 0.7 %copy-done.4 = f32[4,8,128]{2,1,0:T(8,128)S(1)} copy-done((f32[4,8,128]{2,1,0:T(8,128)S(1)}, f32[4,8,128]{2,1,0:T(8,128)}, u32[]{:S(2)}) %copy-start.4) | copy-done | bytes 16408
  4.9 52.2 %invert.1 = (f32[2,16,1024]{2,1,0:T(8,128)S(1)}, f32[2,16,1024]{2,1,0:T(8,128)S(1)}) custom-call(f32[2,32,512]{2,1,0:T(8,128)S(1)} %copy-done.1, f32[4,1024]{1,0:T(4,128)S(1)} %copy-done.3, f32[32,512]{1,0:T(8,128)S(1)} %copy-done.2, bf16[2,768,256]{2,1,0:T(8,128)(2,1)S(1)} %copy-done, f32[4,8,128]{2,1,0:T(8,128)S(1)} %copy-done.4), custom_call_target="tpu_custom_call" | custom-call | tf_op jit(solution)/shard_map/invert/pallas_call | solution.py:515
  57.2 0.7 %copy.9 = f32[2,16,1024]{2,1,0:T(8,128)} copy(f32[2,16,1024]{2,1,0:T(8,128)S(1)} %get-tuple-element.4) | data formatting | bytes 262144
  57.8 0.7 %copy.10 = f32[2,16,1024]{2,1,0:T(8,128)} copy(f32[2,16,1024]{2,1,0:T(8,128)S(1)} %get-tuple-element.5) | data formatting | bytes 262144
Async XLA Ops:
  0.6 1.1 %copy-start = (bf16[2,768,256]{2,1,0:T(8,128)(2,1)S(1)}, bf16[2,768,256]{2,1,0:T(8,128)(2,1)}, u32[]{:S(2)}) copy-start(bf16[2,768,256]{2,1,0:T(8,128)(2,1)} %constant.4.clone.mats_hbm) | copy-start | bytes 2359300
  1.8 0.9 %copy-start.1 = (f32[2,32,512]{2,1,0:T(8,128)S(1)}, f32[2,32,512]{2,1,0:T(8,128)}, u32[]{:S(2)}) copy-start(f32[2,32,512]{2,1,0:T(8,128)} %obs_hbm.1) | copy-start | bytes 393220
  2.7 0.8 %copy-start.2 = (f32[32,512]{1,0:T(8,128)S(1)}, f32[32,512]{1,0:T(8,128)}, u32[]{:S(2)}) copy-start(f32[32,512]{1,0:T(8,128)} %dec_hbm.1) | copy-start | bytes 196612
  3.5 0.7 %copy-start.3 = (f32[4,1024]{1,0:T(4,128)S(1)}, f32[4,1024]{1,0:T(4,128)}, u32[]{:S(2)}) copy-start(f32[4,1024]{1,0:T(4,128)} %win_hbm.1) | copy-start | bytes 49156
  4.2 0.7 %copy-start.4 = (f32[4,8,128]{2,1,0:T(8,128)S(1)}, f32[4,8,128]{2,1,0:T(8,128)}, u32[]{:S(2)}) copy-start(f32[4,8,128]{2,1,0:T(8,128)} %constant.5.clone.tabs_hbm) | copy-start | bytes 49156

commit v2 on v1

v2 whole, which is shorter than its diff:
```python
import functools
import math

import jax
import jax.numpy as jnp
import numpy as np
from jax import lax
from jax.experimental import pallas as pl
from jax.experimental.pallas import tpu as pltpu
from jax.sharding import PartitionSpec as P

MESH = pl.DeviceIdType.MESH
F32 = jnp.float32
BF16 = jnp.bfloat16
GROUP = 32
NX = 4
NZ = 8
RIDGE = 0.5
FLIP = (0, 4, 2, 6, 1, 5, 3, 7)


def tables():
    lane = np.arange(128)
    k2 = 4 * (lane % 32) + lane // 32
    n2 = np.arange(128)
    angle = 2.0 * np.pi * ((k2[:, None] * n2[None, :]) % 128) / 128.0
    cos, sin = np.cos(angle) / 32.0, np.sin(angle) / 32.0
    inverse = np.block([[cos, sin], [-sin, cos]])

    mats = np.stack([inverse, inverse.T]).astype(np.float32)
    turn = 2.0 * np.pi * np.array(FLIP)[:, None] * n2[None, :] / 1024.0
    eighth = 2.0 * np.pi * np.maximum(np.arange(8) - 4, 0) / 8.0
    eighth = np.broadcast_to(eighth[:, None], (8, 128))
    tabs = np.stack([np.cos(turn), np.sin(turn), np.cos(eighth), np.sin(eighth)])
    return mats, tabs.astype(np.float32)


def kernel(
    obs_hbm, win_hbm, dec_hbm, mats_hbm, tabs_hbm, sol_ref, res_ref,
    obs_v, win_v, dec_v, full_v, tabs_v, mats_v, stage_o, stage_d, got_o, got_d,
    spec, dec, carry_x, carry_z, xb, zb, cx, cz,
    in_sem, own_sem, o_send, o_recv, d_send, d_recv, xc_send, xc_recv,
    zc_send, zc_recv, x_send, x_recv, z_send, z_recv,
):
    me = lax.axis_index("chan")
    mz = me // NX
    mx = lax.rem(me, NX)
    barrier = pltpu.get_barrier_semaphore()
    for t in range(1, GROUP):
        pl.semaphore_signal(
            barrier, inc=1, device_id={"chan": lax.rem(me + t, GROUP)}, device_id_type=MESH
        )
    inputs = []
    for t, (src, dst) in enumerate(
        ((obs_hbm, obs_v), (dec_hbm, dec_v), (win_hbm, win_v), (mats_hbm, full_v), (tabs_hbm, tabs_v))
    ):
        copy = pltpu.make_async_copy(src, dst, in_sem.at[t])
        copy.start()
        inputs.append(copy)
    inputs[0].wait()
    inputs[1].wait()

    frames = 512
    lane = lax.broadcasted_iota(jnp.int32, (32, frames), 1)
    row = lax.rem(lax.broadcasted_iota(jnp.int32, (32, frames), 0), 8)

    def shift(value, steps):
        return pltpu.roll(value, steps % frames, axis=value.ndim - 1)

    a = dec_v[...]
    gain = 1.0 - a
    data = [obs_v[0], obs_v[1]]
    prod = jnp.where(lane == 0, 0.0, a)
    run = [gain * d for d in data]
    step = 1
    while step < frames:
        run = [r + prod * shift(r, step) for r in run]
        prod = prod * shift(prod, step)
        step *= 2
    first = [d + 2.0 * r for d, r in zip(data, run)]
    prod = jnp.where(lane == frames - 1, 0.0, shift(a, -1))
    run = first
    step = 1
    while step < frames:
        run = [r + prod * shift(r, -step) for r in run]
        prod = prod * shift(prod, -step)
        step *= 2
    white = [f + 2.0 * gain * r for f, r in zip(first, run)]

    up = (row == 1) | (row == 3)
    down = (row == 4) | (row == 6)

    def flipped(value):
        return jnp.where(
            up,
            pltpu.roll(value, 29, axis=0),
            jnp.where(down, pltpu.roll(value, 3, axis=0), value),
        )

    def moved(value, offset):
        moved_value = shift(value, -offset)
        inside = (lane + offset >= 0) & (lane + offset < frames)
        return jnp.where(inside, moved_value, 0.0)

    white = [flipped(w) for w in white]
    af = flipped(a)
    packed = jnp.concatenate(
        [moved(white[0], -6), moved(white[1], -6), moved(white[0], 10), moved(white[1], 10)], axis=0
    )
    stage_o[...] = packed.T.reshape(GROUP, 16, 128)
    packed = jnp.concatenate([moved(af, 8 * t - 6) for t in range(4)], axis=0)
    stage_d[...] = packed.T.reshape(GROUP, 16, 128)[:, :8]

    pl.semaphore_wait(barrier, GROUP - 1)

    others = sorted(
        ((dz, dx) for dz in range(NZ) for dx in range(NX) if dz or dx),
        key=lambda o: -min(o[0], NZ - o[0]) - min(o[1], NX - o[1]),
    )
    spreads = []
    for stage, got, send, recv in ((stage_d, got_d, d_send, d_recv), (stage_o, got_o, o_send, o_recv)):
        copies = []
        for t, (dz, dx) in enumerate(others):
            to = lax.rem(mz + dz, NZ) * NX + lax.rem(mx + dx, NX)
            copy = pltpu.make_async_remote_copy(
                src_ref=stage.at[to], dst_ref=got.at[:, me, :], send_sem=send.at[t], recv_sem=recv.at[t],
                device_id={"chan": to}, device_id_type=MESH,
            )
            copy.start()
            copies.append(copy)
        spreads.append(copies)
    own = [
        pltpu.make_async_copy(stage_d.at[me], got_d.at[:, me, :], own_sem.at[0]),
        pltpu.make_async_copy(stage_o.at[me], got_o.at[:, me, :], own_sem.at[1]),
    ]
    for copy in own:
        copy.start()
    for copy in inputs[2:]:
        copy.wait()

    for which in range(2):
        full = full_v[which]
        high = full.astype(BF16)
        mats_v[which, 0:256] = high
        mats_v[which, 256:512] = high
        mats_v[which, 512:768] = (full - high.astype(F32)).astype(BF16)

    win = [
        jnp.concatenate([win_v[p : p + 1, n * 128 : (n + 1) * 128] for n in range(8)], axis=0)
        for p in range(4)
    ]

    def butterfly(value, distance):
        index = lax.broadcasted_iota(jnp.int32, value.shape, 1)
        high = (index & distance) != 0
        if distance == 4:
            other = pltpu.roll(value, 4, axis=1)
        else:
            other = jnp.where(
                high, pltpu.roll(value, distance, axis=1), pltpu.roll(value, 8 - distance, axis=1)
            )
        return jnp.where(high, other - value, other + value)

    def quarter(re, im, sign):
        index = lax.broadcasted_iota(jnp.int32, re.shape, 1)
        turned = (index & 3) == 3
        return jnp.where(turned, -sign * im, re), jnp.where(turned, sign * re, im)

    def times(re, im, c, s):
        return re * c - im * s, re * s + im * c

    def product(re, im, which):
        count = re.shape[0]
        x = jnp.concatenate([re.reshape(count * 8, 128), im.reshape(count * 8, 128)], axis=1)
        high = x.astype(BF16)
        low = (x - high.astype(F32)).astype(BF16)
        y = jnp.dot(
            jnp.concatenate([high, low, high], axis=1), mats_v[which], preferred_element_type=F32
        )
        return y[:, :128].reshape(count, 8, 128), y[:, 128:].reshape(count, 8, 128)

    def to_wave(re, im):
        re, im = product(re, im, 0)
        re, im = times(re, im, tabs_v[0], tabs_v[1])
        re, im = butterfly(re, 1), butterfly(im, 1)
        re, im = quarter(re, im, 1.0)
        re, im = butterfly(re, 2), butterfly(im, 2)
        re, im = times(re, im, tabs_v[2], tabs_v[3])
        return butterfly(re, 4), butterfly(im, 4)

    def to_spec(re, im):
        re, im = butterfly(re, 4), butterfly(im, 4)
        re, im = times(re, im, tabs_v[2], -tabs_v[3])
        re, im = butterfly(re, 2), butterfly(im, 2)
        re, im = quarter(re, im, -1.0)
        re, im = butterfly(re, 1), butterfly(im, 1)
        re, im = times(re, im, tabs_v[0], -tabs_v[1])
        return product(re, im, 1)

    def gather_taps(u, count):
        out = win[0] * u[0:count]
        for p in range(1, 4):
            out = out + win[p] * u[p : p + count]
        return out

    def spread_taps(v, count):
        out = win[0] * v[3 : 3 + count]
        for p in range(1, 4):
            out = out + win[p] * v[3 - p : 3 - p + count]
        return out

    def keep(value, start, before, after):
        index = lax.broadcasted_iota(jnp.int32, value.shape, 0) + start
        out = value
        if before:
            out = jnp.where((index < 6) & (me == 0), 0.0, out)
        if after:
            out = jnp.where((index >= 22) & (me == GROUP - 1), 0.0, out)
        return out

    own[0].wait()
    for copy in spreads[0]:
        copy.wait_recv()

    lane8 = lax.broadcasted_iota(jnp.int32, (8, 128), 1)
    low64 = lane8 < 64
    low32 = (lane8 & 32) == 0

    def exchange(v):
        y = [None] * 4
        for i in range(2):
            y[i] = jnp.where(low64, v[i], pltpu.roll(v[i + 2], 64, axis=1))
            y[i + 2] = jnp.where(low64, pltpu.roll(v[i], 64, axis=1), v[i + 2])
        z = [None] * 4
        for i in (0, 2):
            z[i] = jnp.where(low32, y[i], pltpu.roll(y[i + 1], 32, axis=1))
            z[i + 1] = jnp.where(low32, pltpu.roll(y[i], 96, axis=1), y[i + 1])
        return z

    for q in range(2):
        turned = got_d[4 * q : 4 * q + 4].reshape(128, 128).T
        for part in range(4):
            base = part * 32
            out = exchange([turned[base + 8 * i : base + 8 * i + 8] for i in range(4)])
            for r in range(4):
                dec[8 * part + 4 * q + r] = out[r]

    def coefficients(start, count):
        stop = start + count
        p = dec[start]
        ps = [p]
        for g in range(start + 1, stop):
            p = dec[g] * p
            ps.append(p)
        b = dec[stop]
        h = ps[-1]
        bs, hs = [b], [h]
        for g in range(stop - 2, start - 1, -1):
            b = dec[g + 1] * b
            h = ps[g - start] + dec[g + 1] * h
            bs.append(b)
            hs.append(h)
        bs.reverse()
        hs.reverse()
        two_p = jnp.stack([2.0 * v for v in ps])
        gains = [2.0 * (1.0 - dec[g]) for g in range(start, stop)]
        left = jnp.stack([2.0 * x + 2.0 * y * z for x, y, z in zip(ps, gains, hs)])
        right = jnp.stack([y * z for y, z in zip(gains, bs)])
        square = sum(4.0 * ps[g - start] * ps[g - start] for g in range(6, 22))
        return two_p, left, right, (ps[15], square, bs[count - 16], 2.0 * hs[count - 16])

    two_p0, left0, right0, coefs0 = coefficients(3, 25)
    two_p1, left1, right1, coefs1 = coefficients(6, 19)
    for turn, coefs in enumerate((coefs0, coefs1)):
        for n, value in enumerate(coefs):
            cx[turn, mx, 8 * n : 8 * n + 8] = value

    sent = spreads[0] + spreads[1]
    sent_left = []

    def x_copies(part, send, recv):
        out = []
        for t in range(1, NX):
            to = mz * NX + lax.rem(mx + t, NX)
            out.append(pltpu.make_async_remote_copy(
                src_ref=part, dst_ref=part, send_sem=send.at[t], recv_sem=recv.at[t],
                device_id={"chan": to}, device_id_type=MESH,
            ))
        for copy in out:
            copy.start()
        sent.extend(out)
        return out

    def z_copies(part, send, recv, left_only=False):
        out = []
        for t in (4, 3, 5, 2, 6, 1, 7):
            to = lax.rem(mz + t, NZ) * NX + mx
            copy = pltpu.make_async_remote_copy(
                src_ref=part, dst_ref=part, send_sem=send.at[t], recv_sem=recv.at[t],
                device_id={"chan": to}, device_id_type=MESH,
            )
            if left_only:
                pl.when(mz + t >= NZ)(copy.start)
                sent_left.append((t, copy))
            else:
                copy.start()
                sent.append(copy)
            out.append((t, copy))
        return out

    def wait_left(copies):
        for t, copy in copies:
            pl.when(mz < t)(copy.wait_recv)

    def wait_all(copies):
        for _, copy in copies:
            copy.wait_recv()

    x_coefs = [x_copies(cx.at[0, mx], xc_send.at[0], xc_recv.at[0]), None]

    own[1].wait()
    for copy in spreads[1]:
        copy.wait_recv()

    for q in range(4):
        turned = got_o[4 * q : 4 * q + 4].reshape(128, 128).T
        for half in range(2):
            for c in range(2):
                base = half * 64 + c * 32
                out = exchange([turned[base + 8 * i : base + 8 * i + 8] for i in range(4)])
                for r in range(4):
                    spec[c, 16 * half + 4 * q + r] = out[r]

    def local_whiten(re, im, start, count):
        stop = start + count
        x = [jnp.stack([re[g], im[g]]) for g in range(count)]
        s = (1.0 - dec[start]) * x[0]
        e = [x[0] + 2.0 * s]
        leaving_right = None
        for g in range(1, count):
            a = dec[start + g]
            s = a * s + (1.0 - a) * x[g]
            e.append(x[g] + 2.0 * s)
            if g == 15:
                leaving_right = s
        back = e[-1]
        w = [None] * count
        leaving_left = None
        w[-1] = e[-1] + 2.0 * (1.0 - dec[stop - 1]) * back
        for g in range(count - 2, -1, -1):
            back = e[g] + dec[start + g + 1] * back
            w[g] = e[g] + 2.0 * (1.0 - dec[start + g]) * back
            if g == count - 16:
                leaving_left = back
        return e, w, leaving_right, leaving_left

    def chain(carry, back, left, right, a, b, k):
        count = len(left)
        cs = [carry]
        for n in range(count):
            cs.append(a[n] * cs[n] + left[n])
        ds = [None] * count
        d = back
        for n in range(count - 1, -1, -1):
            ds[n] = d
            d = b[n] * d + (right[n] + k[n] * cs[n])
        return cs, ds, d

    def pair(ref, base):
        return jnp.stack([ref[base : base + 8], ref[base + 8 : base + 16]])

    zero = jnp.zeros((2, 8, 128), F32)

    z_coefs = [None, None]

    def group_coefficients(turn):
        for copy in x_coefs[turn]:
            copy.wait_recv()
        a, q, b, k = [[cx[turn, n, 8 * m : 8 * m + 8] for n in range(NX)] for m in range(4)]
        ga, gq, gb, gk = a[0], q[0], b[0], k[0]
        for n in range(1, NX):
            gq = gq + q[n] * (ga * ga)
            gk = gb * k[n] * ga + gk
            gb = gb * b[n]
            ga = a[n] * ga
        for m, value in enumerate((ga, gq, gb, gk)):
            cz[turn, mz, 8 * m : 8 * m + 8] = value
        z_coefs[turn] = (
            z_copies(cz.at[turn, mz, pl.ds(0, 16)], zc_send.at[turn, 0], zc_recv.at[turn, 0]),
            z_copies(cz.at[turn, mz, pl.ds(16, 16)], zc_send.at[turn, 1], zc_recv.at[turn, 1], True),
        )

    def row_sum(value):
        return jnp.sum(value, axis=0, keepdims=True)

    def write_pair(ref, base, value):
        ref[base : base + 8] = value[0]
        ref[base + 8 : base + 16] = value[1]

    def carries(turn, e, two_p, right_going, left_going, row):
        xv = xb.at[turn, mx]
        write_pair(xv, 0, right_going)
        write_pair(xv, 16, left_going)
        x_lh = x_copies(xb.at[turn, mx, pl.ds(0, 32)], x_send.at[turn, 0], x_recv.at[turn, 0])
        linear = sum((2.0 * e[g]) * two_p[g] for g in range(16))
        square = sum(e[g] * e[g] for g in range(16))
        write_pair(xv, 32, linear)
        xv[48:49] = row_sum(square[0] + square[1])
        xv[49:50] = row
        x_rest = x_copies(xb.at[turn, mx, pl.ds(32, 18)], x_send.at[turn, 1], x_recv.at[turn, 1])
        if turn == 0:
            x_coefs[1] = x_copies(cx.at[1, mx], xc_send.at[1], xc_recv.at[1])
            group_coefficients(0)
        a, q, b, k = [[cx[turn, n, 8 * m : 8 * m + 8] for n in range(NX)] for m in range(4)]
        for copy in x_lh:
            copy.wait_recv()
        left = [pair(xb.at[turn, n], 0) for n in range(NX)]
        right = [pair(xb.at[turn, n], 16) for n in range(NX)]
        cs, _, out = chain(zero, zero, left, right, a, b, k)
        zv = zb.at[turn, mz]
        write_pair(zv, 0, cs[NX])
        z_l = z_copies(zb.at[turn, mz, pl.ds(0, 16)], z_send.at[turn, 0], z_recv.at[turn, 0])
        write_pair(zv, 16, out)
        z_h = z_copies(zb.at[turn, mz, pl.ds(16, 16)], z_send.at[turn, 1], z_recv.at[turn, 1], True)
        for copy in x_rest:
            copy.wait_recv()
        linear = [pair(xb.at[turn, n], 32) for n in range(NX)]
        total = linear[0]
        partial = jnp.zeros((8, 128), F32)
        ga = a[0]
        for n in range(1, NX):
            full = linear[n] + q[n] * cs[n]
            partial = partial + full[0] * cs[n][0] + full[1] * cs[n][1]
            total = total + ga * (full + q[n] * cs[n])
            ga = a[n] * ga
        write_pair(zv, 32, total)
        zv[48:49] = row_sum(partial) + sum(xb[turn, n, 48:49] for n in range(NX))
        zv[49:50] = sum(xb[turn, n, 49:50] for n in range(NX))
        z_rest = z_copies(zb.at[turn, mz, pl.ds(32, 18)], z_send.at[turn, 2], z_recv.at[turn, 2])
        if turn == 0:
            group_coefficients(1)
        wait_all(z_coefs[turn][0])
        wait_left(z_coefs[turn][1])
        wait_all(z_l)
        za, zq, zbk, zk = [[cz[turn, n, 8 * m : 8 * m + 8] for n in range(NZ)] for m in range(4)]
        zleft = [pair(zb.at[turn, n], 0) for n in range(NZ)]
        wait_left(z_h)
        zright = [pair(zb.at[turn, n], 16) for n in range(NZ)]
        zcs, zds, _ = chain(zero, zero, zleft, zright, za, zbk, zk)
        for n in range(NZ):
            carry_z[0, n] = zcs[n]
            carry_z[1, n] = zds[n]
        cs, ds, _ = chain(carry_z[0, mz], carry_z[1, mz], left, right, a, b, k)
        for n in range(NX):
            carry_x[0, n] = cs[n]
            carry_x[1, n] = ds[n]

        def sums():
            wait_all(z_rest)
            partial = jnp.zeros((8, 128), F32)
            for n in range(NZ):
                full = (pair(zb.at[turn, n], 32) + zq[n] * zcs[n]) * zcs[n]
                partial = partial + full[0] + full[1]
            squares = row_sum(partial) + sum(zb[turn, n, 48:49] for n in range(NZ))
            rows = sum(zb[turn, n, 49:50] for n in range(NZ))
            return jnp.sum(squares, axis=1, keepdims=True), jnp.sum(rows, axis=1, keepdims=True)

        return carry_x[0, mx], carry_x[1, mx], sums

    def corrected(w, left, right, c, d):
        re = jnp.stack([v[0] for v in w]) + left * c[0] + right * d[0]
        im = jnp.stack([v[1] for v in w]) + left * c[1] + right * d[1]
        return re, im

    def padded(re, im):
        fill = jnp.zeros((1, 8, 128), F32)
        return jnp.concatenate([re, fill]), jnp.concatenate([im, fill])

    def squares(value):
        return row_sum(jnp.sum(value[0] * value[0] + value[1] * value[1], axis=0))

    u = to_wave(spec[0], spec[1])
    r0 = [keep(gather_taps(v, 29), 0, True, False) for v in u]
    x = to_spec(*[spread_taps(v, 26) for v in r0])
    x0 = [keep(v, 3, False, True) for v in x]
    mine_r0 = [v[6:22] for v in r0]
    e, w, going_right, going_left = local_whiten(x0[0], x0[1], 3, 25)
    c, d, sums = carries(0, e[3:19], two_p0[3:19], going_right, going_left, squares(mine_r0))
    w = corrected(w, left0, right0, c, d)

    u = to_wave(*padded(*w))
    q1 = [
        keep(gather_taps(v, 22) + RIDGE * r[3:25], 3, True, False) for v, r in zip(u, r0)
    ]
    x = to_spec(*padded(*[spread_taps(v, 19) for v in q1]))
    energy, rr = sums()
    alpha = rr / (energy + RIDGE * rr)
    x1 = [b[3:22] - alpha * keep(v[:19], 6, False, True) for b, v in zip(x0, x)]
    mine_q1 = [v[3:19] for v in q1]
    r1 = [r - alpha * q for r, q in zip(mine_r0, mine_q1)]
    e, w, going_right, going_left = local_whiten(x1[0], x1[1], 6, 19)
    c, d, sums = carries(1, e[:16], two_p1[:16], going_right, going_left, squares(r1))
    w = corrected(w, left1, right1, c, d)

    u = to_wave(*padded(*w))
    n1 = [gather_taps(v, 16) + RIDGE * r for v, r in zip(u, r1)]
    energy, new = sums()
    beta = new / rr
    alpha_next = new / (energy + RIDGE * new - beta * new / alpha)
    for n in range(2):
        direction = r1[n] + beta * mine_r0[n]
        image = n1[n] + beta * mine_q1[n]
        sol = alpha * mine_r0[n] + alpha_next * direction
        res = r1[n] - alpha_next * image
        sol_ref[n] = sol.reshape(16, 1024)
        res_ref[n] = res.reshape(16, 1024)
    for copy in sent:
        copy.wait_send()
    for t, copy in sent_left:
        pl.when(mz + t >= NZ)(copy.wait_send)


def body(observed, window, decays):
    mats, tabs = tables()
    any_space = pl.BlockSpec(memory_space=pltpu.HBM)
    vmem = pl.BlockSpec(memory_space=pltpu.VMEM)
    dma = pltpu.SemaphoreType.DMA
    out = jax.ShapeDtypeStruct((2, 16, 1024), F32)
    return pl.pallas_call(
        kernel,
        out_shape=(out, out),
        in_specs=[any_space] * 5,
        out_specs=(vmem, vmem),
        scratch_shapes=[
            pltpu.VMEM((2, 32, 512), F32),
            pltpu.VMEM((4, 1024), F32),
            pltpu.VMEM((32, 512), F32),
            pltpu.VMEM((2, 256, 256), F32),
            pltpu.VMEM((4, 8, 128), F32),
            pltpu.VMEM((2, 768, 256), BF16),
            pltpu.VMEM((GROUP, 16, 128), F32),
            pltpu.VMEM((GROUP, 8, 128), F32),
            pltpu.VMEM((16, GROUP, 128), F32),
            pltpu.VMEM((8, GROUP, 128), F32),
            pltpu.VMEM((2, 32, 8, 128), F32),
            pltpu.VMEM((32, 8, 128), F32),
            pltpu.VMEM((2, NX, 2, 8, 128), F32),
            pltpu.VMEM((2, NZ, 2, 8, 128), F32),
            pltpu.VMEM((2, NX, 56, 128), F32),
            pltpu.VMEM((2, NZ, 56, 128), F32),
            pltpu.VMEM((2, NX, 32, 128), F32),
            pltpu.VMEM((2, NZ, 32, 128), F32),
            dma((5,)),
            dma((2,)),
            dma((GROUP,)), dma((GROUP,)),
            dma((GROUP,)), dma((GROUP,)),
            dma((2, NX)), dma((2, NX)),
            dma((2, 2, NZ)), dma((2, 2, NZ)),
            dma((2, 2, NX)), dma((2, 2, NX)),
            dma((2, 3, NZ)), dma((2, 3, NZ)),
        ],
        name="invert",
        compiler_params=pltpu.CompilerParams(
            collective_id=0, has_side_effects=True, vmem_limit_bytes=48 * 1024 * 1024
        ),
    )(*[pltpu.with_memory_space_constraint(v, pltpu.HBM) for v in (observed, window, decays, jnp.asarray(mats), jnp.asarray(tabs))])


def solution(mesh):
    return jax.shard_map(
        body,
        mesh=mesh,
        in_specs=(P(None, "chan", "beam"), P(), P("chan", "beam")),
        out_specs=(P(None, ("beam", "chan"), None), P(None, ("beam", "chan"), None)),
        check_vma=False,
    )
```

time: 58.8 us -> 47.9 us (0.81)
  Pallas kernels: 52.2 us -> 45.8 us
  local copies, waits for them, and re-layouts: 5.62 us -> 1.31 us
    pallas_call x1, Pallas kernels: 52.2 us -> 45.8 us  [body(): pl.pallas_call(kernel, out_shape=(out, out), in_specs=[any_space] * 5, ou...]
    unnamed x12 -> x2, local copies, waits for them, and re-layouts: 5.62 us -> 1.31 us
where the time goes in v2:
time: 47.9 us; the launch traced here: 47.8 us
  Pallas kernels  45.8 us (96%)
  local copies, waits for them, and re-layouts  1.31 us (3%)
  between operations  0.64 us (1%)
    pallas_call x1, Pallas kernels, body(): pl.pallas_call(kernel, out_shape=(out, out), in_specs=[any_space] * 5, ou...  45.8 us
    unnamed x2, local copies, waits for them, and re-layouts  1.31 us

profile of v2, /device:TPU:8, one launch (start us, length us, event | category | flops | bytes accessed | tf_op | source)
XLA Modules:
  0.0 47.8 jit_solution(10510091975526837108)
XLA Ops:
  0.6 45.8 %invert.1 = (f32[2,16,1024]{2,1,0:T(8,128)S(1)}, f32[2,16,1024]{2,1,0:T(8,128)S(1)}) custom-call(f32[2,32,512]{2,1,0:T(8,128)} %obs_hbm.1, f32[4,1024]{1,0:T(4,128)} %win_hbm.1, f32[32,512]{1,0:T(8,128)} %dec_hbm.1, f32[2,256,256]{2,1,0:T(8,128)} %constant.4.clone.mats_hbm, f32[4,8,128]{2,1,0:T(8,128)} %constant.5.clone.tabs_hbm), custom_call_target="tpu_custom_call" | custom-call | tf_op jit(solution)/shard_map/invert/pallas_call | solution.py:529
  46.5 0.7 %copy.9 = f32[2,16,1024]{2,1,0:T(8,128)} copy(f32[2,16,1024]{2,1,0:T(8,128)S(1)} %get-tuple-element.4) | data formatting | bytes 262144
  47.1 0.7 %copy.10 = f32[2,16,1024]{2,1,0:T(8,128)} copy(f32[2,16,1024]{2,1,0:T(8,128)S(1)} %get-tuple-element.5) | data formatting | bytes 262144

commit v3 on v2

--- a/solution.py
+++ b/solution.py
@@ -245,38 +245,39 @@
             for r in range(4):
                 dec[8 * part + 4 * q + r] = out[r]
 
-    def coefficients(start, count):
-        stop = start + count
-        p = dec[start]
-        ps = [p]
-        for g in range(start + 1, stop):
-            p = dec[g] * p
-            ps.append(p)
-        b = dec[stop]
-        h = ps[-1]
-        bs, hs = [b], [h]
-        for g in range(stop - 2, start - 1, -1):
-            b = dec[g + 1] * b
-            h = ps[g - start] + dec[g + 1] * h
-            bs.append(b)
-            hs.append(h)
-        bs.reverse()
-        hs.reverse()
-        two_p = jnp.stack([2.0 * v for v in ps])
-        gains = [2.0 * (1.0 - dec[g]) for g in range(start, stop)]
-        left = jnp.stack([2.0 * x + 2.0 * y * z for x, y, z in zip(ps, gains, hs)])
-        right = jnp.stack([y * z for y, z in zip(gains, bs)])
-        square = sum(4.0 * ps[g - start] * ps[g - start] for g in range(6, 22))
-        return two_p, left, right, (ps[15], square, bs[count - 16], 2.0 * hs[count - 16])
-
-    two_p0, left0, right0, coefs0 = coefficients(3, 25)
-    two_p1, left1, right1, coefs1 = coefficients(6, 19)
-    for turn, coefs in enumerate((coefs0, coefs1)):
-        for n, value in enumerate(coefs):
-            cx[turn, mx, 8 * n : 8 * n + 8] = value
+    def inverse(a):
+        return jnp.where(a > 0.0, 1.0 / jnp.where(a > 0.0, a, 1.0), 0.0)
+
+    def backward(e, start, stop):
+        g = {21: e[21]}
+        for f in range(20, start - 1, -1):
+            g[f] = e[f] + dec[f + 1] * g[f + 1]
+        if stop > 22:
+            g[22] = jnp.zeros_like(e[21])
+        for f in range(23, stop):
+            g[f] = (g[f - 1] - e[f - 1]) * inv[f]
+        return g
+
+    inv = {f: inverse(dec[f]) for f in (4, 5, 22, 23, 24, 25, 26, 27)}
+    twice = {f: 2.0 * (1.0 - dec[f]) for f in range(3, 28)}
+    prods = {5: jnp.ones((8, 128), F32)}
+    for f in range(6, 28):
+        prods[f] = dec[f] * prods[f - 1]
+    prods[4] = inv[5]
+    prods[3] = inv[4] * inv[5]
+    from_c = {f: 2.0 * prods[f] for f in range(3, 28)}
+    back_c = backward(from_c, 3, 28)
+    back_d = {21: jnp.ones((8, 128), F32), 22: inv[22]}
+    for f in range(20, 2, -1):
+        back_d[f] = dec[f + 1] * back_d[f + 1]
+    for f in range(23, 28):
+        back_d[f] = back_d[f - 1] * inv[f]
+    left_all = jnp.stack([from_c[f] + twice[f] * back_c[f] for f in range(3, 28)])
+    right_all = jnp.stack([twice[f] * back_d[f] for f in range(3, 28)])
+    cx[mx, 0:8] = prods[21]
+    cx[mx, 8:16] = dec[6] * back_c[6]
 
     sent = spreads[0] + spreads[1]
-    sent_left = []
 
     def x_copies(part, send, recv):
         out = []
@@ -291,32 +292,24 @@
         sent.extend(out)
         return out
 
-    def z_copies(part, send, recv, left_only=False):
+    def z_copies(part, send, recv):
         out = []
         for t in (4, 3, 5, 2, 6, 1, 7):
             to = lax.rem(mz + t, NZ) * NX + mx
-            copy = pltpu.make_async_remote_copy(
+            out.append(pltpu.make_async_remote_copy(
                 src_ref=part, dst_ref=part, send_sem=send.at[t], recv_sem=recv.at[t],
                 device_id={"chan": to}, device_id_type=MESH,
-            )
-            if left_only:
-                pl.when(mz + t >= NZ)(copy.start)
-                sent_left.append((t, copy))
-            else:
-                copy.start()
-                sent.append(copy)
-            out.append((t, copy))
+            ))
+        for copy in out:
+            copy.start()
+        sent.extend(out)
         return out
 
-    def wait_left(copies):
-        for t, copy in copies:
-            pl.when(mz < t)(copy.wait_recv)
-
     def wait_all(copies):
-        for _, copy in copies:
+        for copy in copies:
             copy.wait_recv()
 
-    x_coefs = [x_copies(cx.at[0, mx], xc_send.at[0], xc_recv.at[0]), None]
+    x_coefs = x_copies(cx.at[mx], xc_send, xc_recv)
 
     own[1].wait()
     for copy in spreads[1]:
@@ -331,30 +324,19 @@
                 for r in range(4):
                     spec[c, 16 * half + 4 * q + r] = out[r]
 
-    def local_whiten(re, im, start, count):
-        stop = start + count
-        x = [jnp.stack([re[g], im[g]]) for g in range(count)]
-        s = (1.0 - dec[start]) * x[0]
-        e = [x[0] + 2.0 * s]
-        leaving_right = None
-        for g in range(1, count):
-            a = dec[start + g]
-            s = a * s + (1.0 - a) * x[g]
-            e.append(x[g] + 2.0 * s)
-            if g == 15:
-                leaving_right = s
-        back = e[-1]
-        w = [None] * count
-        leaving_left = None
-        w[-1] = e[-1] + 2.0 * (1.0 - dec[stop - 1]) * back
-        for g in range(count - 2, -1, -1):
-            back = e[g] + dec[start + g + 1] * back
-            w[g] = e[g] + 2.0 * (1.0 - dec[start + g]) * back
-            if g == count - 16:
-                leaving_left = back
-        return e, w, leaving_right, leaving_left
-
-    def chain(carry, back, left, right, a, b, k):
+    def local_whiten(re, im, start, stop):
+        x = {f: jnp.stack([re[f - start], im[f - start]]) for f in range(start, stop)}
+        s = {5: jnp.zeros((2, 8, 128), F32)}
+        for f in range(6, stop):
+            s[f] = dec[f] * s[f - 1] + (1.0 - dec[f]) * x[f]
+        for f in range(4, start - 1, -1):
+            s[f] = (s[f + 1] - (1.0 - dec[f + 1]) * x[f + 1]) * inv[f + 1]
+        e = {f: x[f] + 2.0 * s[f] for f in range(start, stop)}
+        g = backward(e, start, stop)
+        w = [e[f] + twice[f] * g[f] for f in range(start, stop)]
+        return e, w, s[21], dec[6] * g[6]
+
+    def chain(carry, back, left, right, a, k):
         count = len(left)
         cs = [carry]
         for n in range(count):
@@ -363,32 +345,13 @@
         d = back
         for n in range(count - 1, -1, -1):
             ds[n] = d
-            d = b[n] * d + (right[n] + k[n] * cs[n])
+            d = a[n] * d + (right[n] + k[n] * cs[n])
         return cs, ds, d
 
     def pair(ref, base):
         return jnp.stack([ref[base : base + 8], ref[base + 8 : base + 16]])
 
     zero = jnp.zeros((2, 8, 128), F32)
-
-    z_coefs = [None, None]
-
-    def group_coefficients(turn):
-        for copy in x_coefs[turn]:
-            copy.wait_recv()
-        a, q, b, k = [[cx[turn, n, 8 * m : 8 * m + 8] for n in range(NX)] for m in range(4)]
-        ga, gq, gb, gk = a[0], q[0], b[0], k[0]
-        for n in range(1, NX):
-            gq = gq + q[n] * (ga * ga)
-            gk = gb * k[n] * ga + gk
-            gb = gb * b[n]
-            ga = a[n] * ga
-        for m, value in enumerate((ga, gq, gb, gk)):
-            cz[turn, mz, 8 * m : 8 * m + 8] = value
-        z_coefs[turn] = (
-            z_copies(cz.at[turn, mz, pl.ds(0, 16)], zc_send.at[turn, 0], zc_recv.at[turn, 0]),
-            z_copies(cz.at[turn, mz, pl.ds(16, 16)], zc_send.at[turn, 1], zc_recv.at[turn, 1], True),
-        )
 
     def row_sum(value):
         return jnp.sum(value, axis=0, keepdims=True)
@@ -397,72 +360,67 @@
         ref[base : base + 8] = value[0]
         ref[base + 8 : base + 16] = value[1]
 
-    def carries(turn, e, two_p, right_going, left_going, row):
+    def crossed(cs, right, k):
+        total = jnp.zeros((8, 128), F32)
+        for c, h, q in zip(cs, right, k):
+            full = (4.0 * h + (2.0 * q) * c) * c
+            total = total + full[0] + full[1]
+        return row_sum(total)
+
+    z_coefs = []
+
+    def group_coefficients():
+        for copy in x_coefs:
+            copy.wait_recv()
+        a, k = [[cx[n, 8 * m : 8 * m + 8] for n in range(NX)] for m in range(2)]
+        ga, gk = a[0], k[0]
+        for n in range(1, NX):
+            gk = gk + k[n] * (ga * ga)
+            ga = a[n] * ga
+        cz[mz, 0:8] = ga
+        cz[mz, 8:16] = gk
+        z_coefs.extend(z_copies(cz.at[mz], zc_send, zc_recv))
+
+    def carries(turn, e, right_going, left_going, row):
         xv = xb.at[turn, mx]
         write_pair(xv, 0, right_going)
         write_pair(xv, 16, left_going)
-        x_lh = x_copies(xb.at[turn, mx, pl.ds(0, 32)], x_send.at[turn, 0], x_recv.at[turn, 0])
-        linear = sum((2.0 * e[g]) * two_p[g] for g in range(16))
-        square = sum(e[g] * e[g] for g in range(16))
-        write_pair(xv, 32, linear)
-        xv[48:49] = row_sum(square[0] + square[1])
-        xv[49:50] = row
-        x_rest = x_copies(xb.at[turn, mx, pl.ds(32, 18)], x_send.at[turn, 1], x_recv.at[turn, 1])
+        square = sum(e[f] * e[f] for f in range(6, 22))
+        xv[32:33] = row_sum(square[0] + square[1])
+        xv[33:34] = row
+        x_all = x_copies(xb.at[turn, mx, pl.ds(0, 34)], x_send.at[turn], x_recv.at[turn])
         if turn == 0:
-            x_coefs[1] = x_copies(cx.at[1, mx], xc_send.at[1], xc_recv.at[1])
-            group_coefficients(0)
-        a, q, b, k = [[cx[turn, n, 8 * m : 8 * m + 8] for n in range(NX)] for m in range(4)]
-        for copy in x_lh:
+            group_coefficients()
+        a, k = [[cx[n, 8 * m : 8 * m + 8] for n in range(NX)] for m in range(2)]
+        for copy in x_all:
             copy.wait_recv()
         left = [pair(xb.at[turn, n], 0) for n in range(NX)]
         right = [pair(xb.at[turn, n], 16) for n in range(NX)]
-        cs, _, out = chain(zero, zero, left, right, a, b, k)
+        cs, _, out = chain(zero, zero, left, right, a, k)
         zv = zb.at[turn, mz]
         write_pair(zv, 0, cs[NX])
-        z_l = z_copies(zb.at[turn, mz, pl.ds(0, 16)], z_send.at[turn, 0], z_recv.at[turn, 0])
         write_pair(zv, 16, out)
-        z_h = z_copies(zb.at[turn, mz, pl.ds(16, 16)], z_send.at[turn, 1], z_recv.at[turn, 1], True)
-        for copy in x_rest:
-            copy.wait_recv()
-        linear = [pair(xb.at[turn, n], 32) for n in range(NX)]
-        total = linear[0]
-        partial = jnp.zeros((8, 128), F32)
-        ga = a[0]
-        for n in range(1, NX):
-            full = linear[n] + q[n] * cs[n]
-            partial = partial + full[0] * cs[n][0] + full[1] * cs[n][1]
-            total = total + ga * (full + q[n] * cs[n])
-            ga = a[n] * ga
-        write_pair(zv, 32, total)
-        zv[48:49] = row_sum(partial) + sum(xb[turn, n, 48:49] for n in range(NX))
-        zv[49:50] = sum(xb[turn, n, 49:50] for n in range(NX))
-        z_rest = z_copies(zb.at[turn, mz, pl.ds(32, 18)], z_send.at[turn, 2], z_recv.at[turn, 2])
+        zv[32:33] = crossed(cs[:NX], right, k) + sum(xb[turn, n, 32:33] for n in range(NX))
+        zv[33:34] = sum(xb[turn, n, 33:34] for n in range(NX))
+        z_all = z_copies(zb.at[turn, mz, pl.ds(0, 34)], z_send.at[turn], z_recv.at[turn])
         if turn == 0:
-            group_coefficients(1)
-        wait_all(z_coefs[turn][0])
-        wait_left(z_coefs[turn][1])
-        wait_all(z_l)
-        za, zq, zbk, zk = [[cz[turn, n, 8 * m : 8 * m + 8] for n in range(NZ)] for m in range(4)]
+            wait_all(z_coefs)
+        za, zk = [[cz[n, 8 * m : 8 * m + 8] for n in range(NZ)] for m in range(2)]
+        wait_all(z_all)
         zleft = [pair(zb.at[turn, n], 0) for n in range(NZ)]
-        wait_left(z_h)
         zright = [pair(zb.at[turn, n], 16) for n in range(NZ)]
-        zcs, zds, _ = chain(zero, zero, zleft, zright, za, zbk, zk)
+        zcs, zds, _ = chain(zero, zero, zleft, zright, za, zk)
         for n in range(NZ):
             carry_z[0, n] = zcs[n]
             carry_z[1, n] = zds[n]
-        cs, ds, _ = chain(carry_z[0, mz], carry_z[1, mz], left, right, a, b, k)
+        cs, ds, _ = chain(carry_z[0, mz], carry_z[1, mz], left, right, a, k)
         for n in range(NX):
             carry_x[0, n] = cs[n]
             carry_x[1, n] = ds[n]
 
         def sums():
-            wait_all(z_rest)
-            partial = jnp.zeros((8, 128), F32)
-            for n in range(NZ):
-                full = (pair(zb.at[turn, n], 32) + zq[n] * zcs[n]) * zcs[n]
-                partial = partial + full[0] + full[1]
-            squares = row_sum(partial) + sum(zb[turn, n, 48:49] for n in range(NZ))
-            rows = sum(zb[turn, n, 49:50] for n in range(NZ))
+            squares = crossed(zcs[:NZ], zright, zk) + sum(zb[turn, n, 32:33] for n in range(NZ))
+            rows = sum(zb[turn, n, 33:34] for n in range(NZ))
             return jnp.sum(squares, axis=1, keepdims=True), jnp.sum(rows, axis=1, keepdims=True)
 
         return carry_x[0, mx], carry_x[1, mx], sums
@@ -484,9 +442,9 @@
     x = to_spec(*[spread_taps(v, 26) for v in r0])
     x0 = [keep(v, 3, False, True) for v in x]
     mine_r0 = [v[6:22] for v in r0]
-    e, w, going_right, going_left = local_whiten(x0[0], x0[1], 3, 25)
-    c, d, sums = carries(0, e[3:19], two_p0[3:19], going_right, going_left, squares(mine_r0))
-    w = corrected(w, left0, right0, c, d)
+    e, w, going_right, going_left = local_whiten(x0[0], x0[1], 3, 28)
+    c, d, sums = carries(0, e, going_right, going_left, squares(mine_r0))
+    w = corrected(w, left_all, right_all, c, d)
 
     u = to_wave(*padded(*w))
     q1 = [
@@ -498,9 +456,9 @@
     x1 = [b[3:22] - alpha * keep(v[:19], 6, False, True) for b, v in zip(x0, x)]
     mine_q1 = [v[3:19] for v in q1]
     r1 = [r - alpha * q for r, q in zip(mine_r0, mine_q1)]
-    e, w, going_right, going_left = local_whiten(x1[0], x1[1], 6, 19)
-    c, d, sums = carries(1, e[:16], two_p1[:16], going_right, going_left, squares(r1))
-    w = corrected(w, left1, right1, c, d)
+    e, w, going_right, going_left = local_whiten(x1[0], x1[1], 6, 25)
+    c, d, sums = carries(1, e, going_right, going_left, squares(r1))
+    w = corrected(w, left_all[3:22], right_all[3:22], c, d)
 
     u = to_wave(*padded(*w))
     n1 = [gather_taps(v, 16) + RIDGE * r for v, r in zip(u, r1)]
@@ -516,8 +474,6 @@
         res_ref[n] = res.reshape(16, 1024)
     for copy in sent:
         copy.wait_send()
-    for t, copy in sent_left:
-        pl.when(mz + t >= NZ)(copy.wait_send)
 
 
 def body(observed, window, decays):
@@ -546,18 +502,18 @@
             pltpu.VMEM((32, 8, 128), F32),
             pltpu.VMEM((2, NX, 2, 8, 128), F32),
             pltpu.VMEM((2, NZ, 2, 8, 128), F32),
-            pltpu.VMEM((2, NX, 56, 128), F32),
-            pltpu.VMEM((2, NZ, 56, 128), F32),
-            pltpu.VMEM((2, NX, 32, 128), F32),
-            pltpu.VMEM((2, NZ, 32, 128), F32),
+            pltpu.VMEM((2, NX, 40, 128), F32),
+            pltpu.VMEM((2, NZ, 40, 128), F32),
+            pltpu.VMEM((NX, 16, 128), F32),
+            pltpu.VMEM((NZ, 16, 128), F32),
             dma((5,)),
             dma((2,)),
             dma((GROUP,)), dma((GROUP,)),
             dma((GROUP,)), dma((GROUP,)),
+            dma((NX,)), dma((NX,)),
+            dma((NZ,)), dma((NZ,)),
             dma((2, NX)), dma((2, NX)),
-            dma((2, 2, NZ)), dma((2, 2, NZ)),
-            dma((2, 2, NX)), dma((2, 2, NX)),
-            dma((2, 3, NZ)), dma((2, 3, NZ)),
+            dma((2, NZ)), dma((2, NZ)),
         ],
         name="invert",
         compiler_params=pltpu.CompilerParams(

time: 47.9 us -> 44.1 us (0.921)
  Pallas kernels: 45.8 us -> 42 us
    pallas_call x1, Pallas kernels: 45.8 us -> 42 us  [body(): pl.pallas_call(kernel, out_shape=(out, out), in_specs=[any_space] * 5, ou...]
where the time goes in v3:
time: 44.1 us; the launch traced here: 44 us
  Pallas kernels  42 us (95%)
  local copies, waits for them, and re-layouts  1.31 us (3%)
  between operations  0.64 us (1%)
    pallas_call x1, Pallas kernels, body(): pl.pallas_call(kernel, out_shape=(out, out), in_specs=[any_space] * 5, ou...  42 us
    unnamed x2, local copies, waits for them, and re-layouts  1.31 us

profile of v3, /device:TPU:8, one launch (start us, length us, event | category | flops | bytes accessed | tf_op | source)
XLA Modules:
  0.0 44.0 jit_solution(11720002926579041914)
XLA Ops:
  0.6 42.0 %invert.1 = (f32[2,16,1024]{2,1,0:T(8,128)S(1)}, f32[2,16,1024]{2,1,0:T(8,128)S(1)}) custom-call(f32[2,32,512]{2,1,0:T(8,128)} %obs_hbm.1, f32[4,1024]{1,0:T(4,128)} %win_hbm.1, f32[32,512]{1,0:T(8,128)} %dec_hbm.1, f32[2,256,256]{2,1,0:T(8,128)} %constant.4.clone.mats_hbm, f32[4,8,128]{2,1,0:T(8,128)} %constant.5.clone.tabs_hbm), custom_call_target="tpu_custom_call" | custom-call | tf_op jit(solution)/shard_map/invert/pallas_call | solution.py:485
  42.7 0.7 %copy.9 = f32[2,16,1024]{2,1,0:T(8,128)} copy(f32[2,16,1024]{2,1,0:T(8,128)S(1)} %get-tuple-element.4) | data formatting | bytes 262144
  43.3 0.7 %copy.10 = f32[2,16,1024]{2,1,0:T(8,128)} copy(f32[2,16,1024]{2,1,0:T(8,128)S(1)} %get-tuple-element.5) | data formatting | bytes 262144

commit v4 on v3

--- a/solution.py
+++ b/solution.py
@@ -36,7 +36,7 @@
 
 
 def kernel(
-    obs_hbm, win_hbm, dec_hbm, mats_hbm, tabs_hbm, sol_ref, res_ref,
+    obs_hbm, win_hbm, dec_hbm, mats_hbm, tabs_hbm, base_ref, mid_ref, drop_ref, share_ref,
     obs_v, win_v, dec_v, full_v, tabs_v, mats_v, stage_o, stage_d, got_o, got_d,
     spec, dec, carry_x, carry_z, xb, zb, cx, cz,
     in_sem, own_sem, o_send, o_recv, d_send, d_recv, xc_send, xc_recv,
@@ -117,18 +117,14 @@
         ((dz, dx) for dz in range(NZ) for dx in range(NX) if dz or dx),
         key=lambda o: -min(o[0], NZ - o[0]) - min(o[1], NX - o[1]),
     )
-    spreads = []
     for stage, got, send, recv in ((stage_d, got_d, d_send, d_recv), (stage_o, got_o, o_send, o_recv)):
-        copies = []
-        for t, (dz, dx) in enumerate(others):
+        for dz, dx in others:
             to = lax.rem(mz + dz, NZ) * NX + lax.rem(mx + dx, NX)
             copy = pltpu.make_async_remote_copy(
-                src_ref=stage.at[to], dst_ref=got.at[:, me, :], send_sem=send.at[t], recv_sem=recv.at[t],
+                src_ref=stage.at[to], dst_ref=got.at[:, me, :], send_sem=send, recv_sem=recv,
                 device_id={"chan": to}, device_id_type=MESH,
             )
             copy.start()
-            copies.append(copy)
-        spreads.append(copies)
     own = [
         pltpu.make_async_copy(stage_d.at[me], got_d.at[:, me, :], own_sem.at[0]),
         pltpu.make_async_copy(stage_o.at[me], got_o.at[:, me, :], own_sem.at[1]),
@@ -218,9 +214,11 @@
             out = jnp.where((index >= 22) & (me == GROUP - 1), 0.0, out)
         return out
 
+    def wait_for(ref, sem):
+        pltpu.make_async_copy(ref, ref, sem).wait()
+
     own[0].wait()
-    for copy in spreads[0]:
-        copy.wait_recv()
+    wait_for(got_d.at[:, pl.ds(0, GROUP - 1)], d_recv)
 
     lane8 = lax.broadcasted_iota(jnp.int32, (8, 128), 1)
     low64 = lane8 < 64
@@ -277,43 +275,33 @@
     cx[mx, 0:8] = prods[21]
     cx[mx, 8:16] = dec[6] * back_c[6]
 
-    sent = spreads[0] + spreads[1]
 
     def x_copies(part, send, recv):
         out = []
         for t in range(1, NX):
             to = mz * NX + lax.rem(mx + t, NX)
             out.append(pltpu.make_async_remote_copy(
-                src_ref=part, dst_ref=part, send_sem=send.at[t], recv_sem=recv.at[t],
+                src_ref=part, dst_ref=part, send_sem=send, recv_sem=recv,
                 device_id={"chan": to}, device_id_type=MESH,
             ))
         for copy in out:
             copy.start()
-        sent.extend(out)
-        return out
 
     def z_copies(part, send, recv):
         out = []
         for t in (4, 3, 5, 2, 6, 1, 7):
             to = lax.rem(mz + t, NZ) * NX + mx
             out.append(pltpu.make_async_remote_copy(
-                src_ref=part, dst_ref=part, send_sem=send.at[t], recv_sem=recv.at[t],
+                src_ref=part, dst_ref=part, send_sem=send, recv_sem=recv,
                 device_id={"chan": to}, device_id_type=MESH,
             ))
         for copy in out:
             copy.start()
-        sent.extend(out)
-        return out
-
-    def wait_all(copies):
-        for copy in copies:
-            copy.wait_recv()
-
-    x_coefs = x_copies(cx.at[mx], xc_send, xc_recv)
+
+    x_copies(cx.at[mx], xc_send, xc_recv)
 
     own[1].wait()
-    for copy in spreads[1]:
-        copy.wait_recv()
+    wait_for(got_o.at[:, pl.ds(0, GROUP - 1)], o_recv)
 
     for q in range(4):
         turned = got_o[4 * q : 4 * q + 4].reshape(128, 128).T
@@ -367,11 +355,8 @@
             total = total + full[0] + full[1]
         return row_sum(total)
 
-    z_coefs = []
-
     def group_coefficients():
-        for copy in x_coefs:
-            copy.wait_recv()
+        wait_for(cx.at[pl.ds(0, NX - 1)], xc_recv)
         a, k = [[cx[n, 8 * m : 8 * m + 8] for n in range(NX)] for m in range(2)]
         ga, gk = a[0], k[0]
         for n in range(1, NX):
@@ -379,7 +364,7 @@
             ga = a[n] * ga
         cz[mz, 0:8] = ga
         cz[mz, 8:16] = gk
-        z_coefs.extend(z_copies(cz.at[mz], zc_send, zc_recv))
+        z_copies(cz.at[mz], zc_send, zc_recv)
 
     def carries(turn, e, right_going, left_going, row):
         xv = xb.at[turn, mx]
@@ -388,12 +373,18 @@
         square = sum(e[f] * e[f] for f in range(6, 22))
         xv[32:33] = row_sum(square[0] + square[1])
         xv[33:34] = row
-        x_all = x_copies(xb.at[turn, mx, pl.ds(0, 34)], x_send.at[turn], x_recv.at[turn])
+        x_copies(xb.at[turn, mx, pl.ds(0, 34)], x_send.at[turn], x_recv.at[turn])
         if turn == 0:
             group_coefficients()
         a, k = [[cx[n, 8 * m : 8 * m + 8] for n in range(NX)] for m in range(2)]
-        for copy in x_all:
-            copy.wait_recv()
+        if turn == 0:
+            wait_for(stage_d.at[pl.ds(0, GROUP - 1)], d_send)
+            wait_for(stage_o.at[pl.ds(0, GROUP - 1)], o_send)
+            wait_for(cx.at[pl.ds(0, NX - 1)], xc_send)
+        else:
+            wait_for(cz.at[pl.ds(0, NZ - 1)], zc_send)
+            wait_for(zb.at[0, pl.ds(0, NZ - 1), pl.ds(0, 34)], z_send.at[0])
+        wait_for(xb.at[turn, pl.ds(0, NX - 1), pl.ds(0, 34)], x_recv.at[turn])
         left = [pair(xb.at[turn, n], 0) for n in range(NX)]
         right = [pair(xb.at[turn, n], 16) for n in range(NX)]
         cs, _, out = chain(zero, zero, left, right, a, k)
@@ -402,11 +393,12 @@
         write_pair(zv, 16, out)
         zv[32:33] = crossed(cs[:NX], right, k) + sum(xb[turn, n, 32:33] for n in range(NX))
         zv[33:34] = sum(xb[turn, n, 33:34] for n in range(NX))
-        z_all = z_copies(zb.at[turn, mz, pl.ds(0, 34)], z_send.at[turn], z_recv.at[turn])
+        z_copies(zb.at[turn, mz, pl.ds(0, 34)], z_send.at[turn], z_recv.at[turn])
         if turn == 0:
-            wait_all(z_coefs)
+            wait_for(cz.at[pl.ds(0, NZ - 1)], zc_recv)
         za, zk = [[cz[n, 8 * m : 8 * m + 8] for n in range(NZ)] for m in range(2)]
-        wait_all(z_all)
+        wait_for(xb.at[turn, pl.ds(0, NX - 1), pl.ds(0, 34)], x_send.at[turn])
+        wait_for(zb.at[turn, pl.ds(0, NZ - 1), pl.ds(0, 34)], z_recv.at[turn])
         zleft = [pair(zb.at[turn, n], 0) for n in range(NZ)]
         zright = [pair(zb.at[turn, n], 16) for n in range(NZ)]
         zcs, zds, _ = chain(zero, zero, zleft, zright, za, zk)
@@ -465,15 +457,13 @@
     energy, new = sums()
     beta = new / rr
     alpha_next = new / (energy + RIDGE * new - beta * new / alpha)
+    share_ref[...] = jnp.broadcast_to(alpha_next, (8, 1024))
     for n in range(2):
-        direction = r1[n] + beta * mine_r0[n]
         image = n1[n] + beta * mine_q1[n]
-        sol = alpha * mine_r0[n] + alpha_next * direction
-        res = r1[n] - alpha_next * image
-        sol_ref[n] = sol.reshape(16, 1024)
-        res_ref[n] = res.reshape(16, 1024)
-    for copy in sent:
-        copy.wait_send()
+        base_ref[n] = ((alpha + alpha_next * beta) * mine_r0[n]).reshape(16, 1024)
+        mid_ref[n] = r1[n].reshape(16, 1024)
+        drop_ref[n] = (alpha_next * image).reshape(16, 1024)
+    wait_for(zb.at[1, pl.ds(0, NZ - 1), pl.ds(0, 34)], z_send.at[1])
 
 
 def body(observed, window, decays):
@@ -482,11 +472,11 @@
     vmem = pl.BlockSpec(memory_space=pltpu.VMEM)
     dma = pltpu.SemaphoreType.DMA
     out = jax.ShapeDtypeStruct((2, 16, 1024), F32)
-    return pl.pallas_call(
+    base, mid, drop, share = pl.pallas_call(
         kernel,
-        out_shape=(out, out),
+        out_shape=(out, out, out, jax.ShapeDtypeStruct((8, 1024), F32)),
         in_specs=[any_space] * 5,
-        out_specs=(vmem, vmem),
+        out_specs=(vmem,) * 4,
         scratch_shapes=[
             pltpu.VMEM((2, 32, 512), F32),
             pltpu.VMEM((4, 1024), F32),
@@ -508,18 +498,15 @@
             pltpu.VMEM((NZ, 16, 128), F32),
             dma((5,)),
             dma((2,)),
-            dma((GROUP,)), dma((GROUP,)),
-            dma((GROUP,)), dma((GROUP,)),
-            dma((NX,)), dma((NX,)),
-            dma((NZ,)), dma((NZ,)),
-            dma((2, NX)), dma((2, NX)),
-            dma((2, NZ)), dma((2, NZ)),
+            dma, dma, dma, dma, dma, dma, dma, dma,
+            dma((2,)), dma((2,)), dma((2,)), dma((2,)),
         ],
         name="invert",
         compiler_params=pltpu.CompilerParams(
             collective_id=0, has_side_effects=True, vmem_limit_bytes=48 * 1024 * 1024
         ),
     )(*[pltpu.with_memory_space_constraint(v, pltpu.HBM) for v in (observed, window, decays, jnp.asarray(mats), jnp.asarray(tabs))])
+    return base + share[:1] * mid, mid - drop
 
 
 def solution(mesh):

time: 44.1 us -> 41.7 us (0.946)
  Pallas kernels: 42 us -> 40.2 us
  local copies, waits for them, and re-layouts: 1.31 us -> 0.01 us
  other arithmetic: 0 us -> 0.73 us
    pallas_call x1, Pallas kernels: 42 us -> 40.2 us  [body(): pl.pallas_call(kernel, out_shape=(out, out, out, jax.ShapeDtypeStruct((8,...]
    unnamed x2 -> x0, local copies, waits for them, and re-layouts: 1.31 us -> none
    sub x0 -> x1, other arithmetic: none -> 0.73 us  [body(): return (base + share[:1] * mid, mid - drop)]
where the time goes in v4:
time: 41.7 us; the launch traced here: 41.6 us
  Pallas kernels  40.2 us (96%)
  other arithmetic  0.73 us (2%)
  between operations  0.65 us (2%)
    pallas_call x1, Pallas kernels, body(): pl.pallas_call(kernel, out_shape=(out, out, out, jax.ShapeDtypeStruct((8,...  40.2 us

profile of v4, /device:TPU:8, one launch (start us, length us, event | category | flops | bytes accessed | tf_op | source)
XLA Modules:
  0.0 41.6 jit_solution(5641696315992040303)
XLA Ops:
  0.6 40.2 %invert.1 = (f32[2,16,1024]{2,1,0:T(8,128)S(1)}, f32[2,16,1024]{2,1,0:T(8,128)S(1)}, f32[2,16,1024]{2,1,0:T(8,128)S(1)}, f32[8,1024]{1,0:T(8,128)S(1)}) custom-call(f32[2,32,512]{2,1,0:T(8,128)} %obs_hbm.1, f32[4,1024]{1,0:T(4,128)} %win_hbm.1, f32[32,512]{1,0:T(8,128)} %dec_hbm.1, f32[2,256,256]{2,1,0:T(8,128)} %constant.4.clone.mats_hbm, ...), custom_call_target="tpu_custom_call" | custom-call | tf_op jit(solution)/shard_map/invert/pallas_call | solution.py:475
  40.9 0.7 %fusion = (f32[2,16,1024]{2,1,0:T(8,128)}, f32[2,16,1024]{2,1,0:T(8,128)}) fusion(f32[2,16,1024]{2,1,0:T(8,128)S(1)} %get-tuple-element.8, f32[2,16,1024]{2,1,0:T(8,128)S(1)} %get-tuple-element.9, f32[2,16,1024]{2,1,0:T(8,128)S(1)} %get-tuple-element.6, f32[1024]{0:T(1024)S(1)} %bitcast.1), kind=kLoop, calls=%fused_computation.1 | loop fusion | flops 98304 | bytes 659456 | tf_op jit(solution)/shard_map/sub | solution.py:509
  (1 shorter events, 0.0 us)

commit v5 on v4

--- a/solution.py
+++ b/solution.py
@@ -38,18 +38,22 @@
 def kernel(
     obs_hbm, win_hbm, dec_hbm, mats_hbm, tabs_hbm, base_ref, mid_ref, drop_ref, share_ref,
     obs_v, win_v, dec_v, full_v, tabs_v, mats_v, stage_o, stage_d, got_o, got_d,
-    spec, dec, carry_x, carry_z, xb, zb, cx, cz,
+    spec, dec, carry_x, carry_z, xb, zb, cx, cz, out_halo, in_halo,
     in_sem, own_sem, o_send, o_recv, d_send, d_recv, xc_send, xc_recv,
     zc_send, zc_recv, x_send, x_recv, z_send, z_recv,
+    h_send, h_recv,
 ):
     me = lax.axis_index("chan")
     mz = me // NX
     mx = lax.rem(me, NX)
     barrier = pltpu.get_barrier_semaphore()
-    for t in range(1, GROUP):
-        pl.semaphore_signal(
-            barrier, inc=1, device_id={"chan": lax.rem(me + t, GROUP)}, device_id_type=MESH
-        )
+    others = sorted(
+        ((dz, dx) for dz in range(NZ) for dx in range(NX) if dz or dx),
+        key=lambda o: -min(o[0], NZ - o[0]) - min(o[1], NX - o[1]),
+    )
+    others = [lax.rem(mz + dz, NZ) * NX + lax.rem(mx + dx, NX) for dz, dx in others]
+    for to in others:
+        pl.semaphore_signal(barrier, inc=1, device_id={"chan": to}, device_id_type=MESH)
     inputs = []
     for t, (src, dst) in enumerate(
         ((obs_hbm, obs_v), (dec_hbm, dec_v), (win_hbm, win_v), (mats_hbm, full_v), (tabs_hbm, tabs_v))
@@ -105,29 +109,27 @@
     white = [flipped(w) for w in white]
     af = flipped(a)
     packed = jnp.concatenate(
-        [moved(white[0], -6), moved(white[1], -6), moved(white[0], 10), moved(white[1], 10)], axis=0
+        [moved(white[0], -3), moved(white[1], -3), moved(white[0], 8), moved(white[1], 8)], axis=0
     )
     stage_o[...] = packed.T.reshape(GROUP, 16, 128)
-    packed = jnp.concatenate([moved(af, 8 * t - 6) for t in range(4)], axis=0)
+    packed = jnp.concatenate([moved(af, 6 * t - 3) for t in range(4)], axis=0)
     stage_d[...] = packed.T.reshape(GROUP, 16, 128)[:, :8]
 
     pl.semaphore_wait(barrier, GROUP - 1)
 
-    others = sorted(
-        ((dz, dx) for dz in range(NZ) for dx in range(NX) if dz or dx),
-        key=lambda o: -min(o[0], NZ - o[0]) - min(o[1], NX - o[1]),
-    )
-    for stage, got, send, recv in ((stage_d, got_d, d_send, d_recv), (stage_o, got_o, o_send, o_recv)):
-        for dz, dx in others:
-            to = lax.rem(mz + dz, NZ) * NX + lax.rem(mx + dx, NX)
+    for stage, got, rows, send, recv in (
+        (stage_d, got_d, 6, d_send, d_recv), (stage_o, got_o, 11, o_send, o_recv)
+    ):
+        for to in others:
             copy = pltpu.make_async_remote_copy(
-                src_ref=stage.at[to], dst_ref=got.at[:, me, :], send_sem=send, recv_sem=recv,
+                src_ref=stage.at[to, pl.ds(0, rows)], dst_ref=got.at[pl.ds(0, rows), me, :],
+                send_sem=send, recv_sem=recv,
                 device_id={"chan": to}, device_id_type=MESH,
             )
             copy.start()
     own = [
-        pltpu.make_async_copy(stage_d.at[me], got_d.at[:, me, :], own_sem.at[0]),
-        pltpu.make_async_copy(stage_o.at[me], got_o.at[:, me, :], own_sem.at[1]),
+        pltpu.make_async_copy(stage_d.at[me, pl.ds(0, 6)], got_d.at[pl.ds(0, 6), me, :], own_sem.at[0]),
+        pltpu.make_async_copy(stage_o.at[me, pl.ds(0, 11)], got_o.at[pl.ds(0, 11), me, :], own_sem.at[1]),
     ]
     for copy in own:
         copy.start()
@@ -147,15 +149,14 @@
     ]
 
     def butterfly(value, distance):
-        index = lax.broadcasted_iota(jnp.int32, value.shape, 1)
-        high = (index & distance) != 0
+        high = (lax.broadcasted_iota(jnp.int32, (8, 128), 0) & distance) != 0
         if distance == 4:
             other = pltpu.roll(value, 4, axis=1)
         else:
             other = jnp.where(
                 high, pltpu.roll(value, distance, axis=1), pltpu.roll(value, 8 - distance, axis=1)
             )
-        return jnp.where(high, other - value, other + value)
+        return other + value * jnp.where(high, -1.0, 1.0)
 
     def quarter(re, im, sign):
         index = lax.broadcasted_iota(jnp.int32, re.shape, 1)
@@ -205,20 +206,15 @@
             out = out + win[p] * v[3 - p : 3 - p + count]
         return out
 
-    def keep(value, start, before, after):
-        index = lax.broadcasted_iota(jnp.int32, value.shape, 0) + start
-        out = value
-        if before:
-            out = jnp.where((index < 6) & (me == 0), 0.0, out)
-        if after:
-            out = jnp.where((index >= 22) & (me == GROUP - 1), 0.0, out)
-        return out
+    def part_only(value):
+        index = lax.broadcasted_iota(jnp.int32, value.shape, 0)
+        return jnp.where((index < 3) & (me == 0), 0.0, value)
 
     def wait_for(ref, sem):
         pltpu.make_async_copy(ref, ref, sem).wait()
 
     own[0].wait()
-    wait_for(got_d.at[:, pl.ds(0, GROUP - 1)], d_recv)
+    wait_for(got_d.at[pl.ds(0, 6), pl.ds(0, GROUP - 1)], d_recv)
 
     lane8 = lax.broadcasted_iota(jnp.int32, (8, 128), 1)
     low64 = lane8 < 64
@@ -240,41 +236,45 @@
         for part in range(4):
             base = part * 32
             out = exchange([turned[base + 8 * i : base + 8 * i + 8] for i in range(4)])
-            for r in range(4):
-                dec[8 * part + 4 * q + r] = out[r]
+            for r in range(min(4, 6 - 4 * q)):
+                dec[6 * part + 4 * q + r] = out[r]
 
     def inverse(a):
         return jnp.where(a > 0.0, 1.0 / jnp.where(a > 0.0, a, 1.0), 0.0)
 
-    def backward(e, start, stop):
-        g = {21: e[21]}
-        for f in range(20, start - 1, -1):
+    def backward(e):
+        g = {18: e[18]}
+        for f in range(17, 2, -1):
             g[f] = e[f] + dec[f + 1] * g[f + 1]
-        if stop > 22:
-            g[22] = jnp.zeros_like(e[21])
-        for f in range(23, stop):
+        return g
+
+    def backward_left(e, g):
+        for f in (2, 1, 0):
+            g[f] = e[f] + dec[f + 1] * g[f + 1]
+
+    def backward_right(e, g):
+        g[19] = jnp.zeros_like(g[18])
+        for f in (20, 21):
             g[f] = (g[f - 1] - e[f - 1]) * inv[f]
-        return g
-
-    inv = {f: inverse(dec[f]) for f in (4, 5, 22, 23, 24, 25, 26, 27)}
-    twice = {f: 2.0 * (1.0 - dec[f]) for f in range(3, 28)}
-    prods = {5: jnp.ones((8, 128), F32)}
-    for f in range(6, 28):
+
+    inv = {f: inverse(dec[f]) for f in (1, 2, 19, 20, 21)}
+    twice = {f: 2.0 * (1.0 - dec[f]) for f in range(22)}
+    prods = {2: jnp.ones((8, 128), F32), 1: inv[2], 0: inv[1] * inv[2]}
+    for f in range(3, 22):
         prods[f] = dec[f] * prods[f - 1]
-    prods[4] = inv[5]
-    prods[3] = inv[4] * inv[5]
-    from_c = {f: 2.0 * prods[f] for f in range(3, 28)}
-    back_c = backward(from_c, 3, 28)
-    back_d = {21: jnp.ones((8, 128), F32), 22: inv[22]}
-    for f in range(20, 2, -1):
+    from_c = {f: 2.0 * prods[f] for f in range(22)}
+    back_c = backward(from_c)
+    backward_left(from_c, back_c)
+    backward_right(from_c, back_c)
+    back_d = {18: jnp.ones((8, 128), F32), 19: inv[19]}
+    for f in range(17, -1, -1):
         back_d[f] = dec[f + 1] * back_d[f + 1]
-    for f in range(23, 28):
+    for f in (20, 21):
         back_d[f] = back_d[f - 1] * inv[f]
-    left_all = jnp.stack([from_c[f] + twice[f] * back_c[f] for f in range(3, 28)])
-    right_all = jnp.stack([twice[f] * back_d[f] for f in range(3, 28)])
-    cx[mx, 0:8] = prods[21]
-    cx[mx, 8:16] = dec[6] * back_c[6]
-
+    left_all = jnp.stack([from_c[f] + twice[f] * back_c[f] for f in range(22)])
+    right_all = jnp.stack([twice[f] * back_d[f] for f in range(22)])
+    cx[mx, 0:8] = prods[18]
+    cx[mx, 8:16] = dec[3] * back_c[3]
 
     def x_copies(part, send, recv):
         out = []
@@ -301,28 +301,57 @@
     x_copies(cx.at[mx], xc_send, xc_recv)
 
     own[1].wait()
-    wait_for(got_o.at[:, pl.ds(0, GROUP - 1)], o_recv)
-
-    for q in range(4):
+    wait_for(got_o.at[pl.ds(0, 11), pl.ds(0, GROUP - 1)], o_recv)
+
+    for q in range(3):
         turned = got_o[4 * q : 4 * q + 4].reshape(128, 128).T
         for half in range(2):
             for c in range(2):
                 base = half * 64 + c * 32
                 out = exchange([turned[base + 8 * i : base + 8 * i + 8] for i in range(4)])
-                for r in range(4):
-                    spec[c, 16 * half + 4 * q + r] = out[r]
-
-    def local_whiten(re, im, start, stop):
-        x = {f: jnp.stack([re[f - start], im[f - start]]) for f in range(start, stop)}
-        s = {5: jnp.zeros((2, 8, 128), F32)}
-        for f in range(6, stop):
-            s[f] = dec[f] * s[f - 1] + (1.0 - dec[f]) * x[f]
-        for f in range(4, start - 1, -1):
-            s[f] = (s[f + 1] - (1.0 - dec[f + 1]) * x[f + 1]) * inv[f + 1]
-        e = {f: x[f] + 2.0 * s[f] for f in range(start, stop)}
-        g = backward(e, start, stop)
-        w = [e[f] + twice[f] * g[f] for f in range(start, stop)]
-        return e, w, s[21], dec[6] * g[6]
+                for r in range(min(4, 11 - 4 * q)):
+                    spec[c, 11 * half + 4 * q + r] = out[r]
+
+    def halo_copy(slot, x, first, to):
+        for n in range(2):
+            for f in range(3):
+                out_halo[slot, n, f] = x[n][first + f]
+        pltpu.make_async_remote_copy(
+            src_ref=out_halo.at[slot], dst_ref=in_halo.at[slot], send_sem=h_send.at[slot], recv_sem=h_recv.at[slot],
+            device_id={"chan": to}, device_id_type=MESH,
+        ).start()
+
+    def halo_frames(slot, outside):
+        wait_for(in_halo.at[slot], h_recv.at[slot])
+        wait_for(out_halo.at[slot], h_send.at[slot])
+        return [
+            jnp.where(outside, 0.0, jnp.stack([in_halo[slot, 0, f], in_halo[slot, 1, f]])) for f in range(3)
+        ]
+
+    def local_whiten(x):
+        s = {2: jnp.zeros((2, 8, 128), F32)}
+        e = {}
+        for f in range(3, 19):
+            own_x = jnp.stack([x[0][f - 3], x[1][f - 3]])
+            s[f] = dec[f] * s[f - 1] + (1.0 - dec[f]) * own_x
+            e[f] = own_x + 2.0 * s[f]
+        return s, e, backward(e)
+
+    def left_whiten(x, s, e, g):
+        for f in (2, 1, 0):
+            if f < 2:
+                s[f] = (s[f + 1] - (1.0 - dec[f + 1]) * x[f + 1]) * inv[f + 1]
+            e[f] = x[f] + 2.0 * s[f]
+        backward_left(e, g)
+
+    def right_whiten(x, s, e, g):
+        for f in (19, 20, 21):
+            s[f] = dec[f] * s[f - 1] + (1.0 - dec[f]) * x[f - 19]
+            e[f] = x[f - 19] + 2.0 * s[f]
+        backward_right(e, g)
+
+    def whole(e, g, start):
+        return [e[f] + twice[f] * g[f] for f in range(start, 22)]
 
     def chain(carry, back, left, right, a, k):
         count = len(left)
@@ -366,20 +395,25 @@
         cz[mz, 8:16] = gk
         z_copies(cz.at[mz], zc_send, zc_recv)
 
-    def carries(turn, e, right_going, left_going, row):
+    def carries(turn, x, row):
+        s, e, g = local_whiten(x)
         xv = xb.at[turn, mx]
-        write_pair(xv, 0, right_going)
-        write_pair(xv, 16, left_going)
-        square = sum(e[f] * e[f] for f in range(6, 22))
+        write_pair(xv, 0, s[18])
+        write_pair(xv, 16, dec[3] * g[3])
+        square = sum(e[f] * e[f] for f in range(3, 19))
         xv[32:33] = row_sum(square[0] + square[1])
         xv[33:34] = row
         x_copies(xb.at[turn, mx, pl.ds(0, 34)], x_send.at[turn], x_recv.at[turn])
         if turn == 0:
+            halo_copy(0, x, 13, lax.rem(me + 1, GROUP))
+            halo_copy(1, x, 0, lax.rem(me + GROUP - 1, GROUP))
             group_coefficients()
+        else:
+            halo_copy(2, x, 0, lax.rem(me + GROUP - 1, GROUP))
         a, k = [[cx[n, 8 * m : 8 * m + 8] for n in range(NX)] for m in range(2)]
         if turn == 0:
-            wait_for(stage_d.at[pl.ds(0, GROUP - 1)], d_send)
-            wait_for(stage_o.at[pl.ds(0, GROUP - 1)], o_send)
+            wait_for(stage_d.at[pl.ds(0, GROUP - 1), pl.ds(0, 6)], d_send)
+            wait_for(stage_o.at[pl.ds(0, GROUP - 1), pl.ds(0, 11)], o_send)
             wait_for(cx.at[pl.ds(0, NX - 1)], xc_send)
         else:
             wait_for(cz.at[pl.ds(0, NZ - 1)], zc_send)
@@ -395,6 +429,10 @@
         zv[33:34] = sum(xb[turn, n, 33:34] for n in range(NX))
         z_copies(zb.at[turn, mz, pl.ds(0, 34)], z_send.at[turn], z_recv.at[turn])
         if turn == 0:
+            left_whiten(halo_frames(0, me == 0), s, e, g)
+        right_whiten(halo_frames(1 + turn, me == GROUP - 1), s, e, g)
+        w = whole(e, g, 3 * turn)
+        if turn == 0:
             wait_for(cz.at[pl.ds(0, NZ - 1)], zc_recv)
         za, zk = [[cz[n, 8 * m : 8 * m + 8] for n in range(NZ)] for m in range(2)]
         wait_for(xb.at[turn, pl.ds(0, NX - 1), pl.ds(0, 34)], x_send.at[turn])
@@ -415,7 +453,7 @@
             rows = sum(zb[turn, n, 33:34] for n in range(NZ))
             return jnp.sum(squares, axis=1, keepdims=True), jnp.sum(rows, axis=1, keepdims=True)
 
-        return carry_x[0, mx], carry_x[1, mx], sums
+        return w, carry_x[0, mx], carry_x[1, mx], sums
 
     def corrected(w, left, right, c, d):
         re = jnp.stack([v[0] for v in w]) + left * c[0] + right * d[0]
@@ -430,27 +468,22 @@
         return row_sum(jnp.sum(value[0] * value[0] + value[1] * value[1], axis=0))
 
     u = to_wave(spec[0], spec[1])
-    r0 = [keep(gather_taps(v, 29), 0, True, False) for v in u]
-    x = to_spec(*[spread_taps(v, 26) for v in r0])
-    x0 = [keep(v, 3, False, True) for v in x]
-    mine_r0 = [v[6:22] for v in r0]
-    e, w, going_right, going_left = local_whiten(x0[0], x0[1], 3, 28)
-    c, d, sums = carries(0, e, going_right, going_left, squares(mine_r0))
+    r0 = [part_only(gather_taps(v, 19)) for v in u]
+    x0 = to_spec(*[spread_taps(v, 16) for v in r0])
+    mine_r0 = [v[3:] for v in r0]
+    w, c, d, sums = carries(0, x0, squares(mine_r0))
     w = corrected(w, left_all, right_all, c, d)
 
-    u = to_wave(*padded(*w))
-    q1 = [
-        keep(gather_taps(v, 22) + RIDGE * r[3:25], 3, True, False) for v, r in zip(u, r0)
-    ]
-    x = to_spec(*padded(*[spread_taps(v, 19) for v in q1]))
+    u = to_wave(*w)
+    q1 = [part_only(gather_taps(v, 19) + RIDGE * r) for v, r in zip(u, r0)]
+    x = to_spec(*[spread_taps(v, 16) for v in q1])
     energy, rr = sums()
     alpha = rr / (energy + RIDGE * rr)
-    x1 = [b[3:22] - alpha * keep(v[:19], 6, False, True) for b, v in zip(x0, x)]
-    mine_q1 = [v[3:19] for v in q1]
+    x1 = [b - alpha * v for b, v in zip(x0, x)]
+    mine_q1 = [v[3:] for v in q1]
     r1 = [r - alpha * q for r, q in zip(mine_r0, mine_q1)]
-    e, w, going_right, going_left = local_whiten(x1[0], x1[1], 6, 25)
-    c, d, sums = carries(1, e, going_right, going_left, squares(r1))
-    w = corrected(w, left_all[3:22], right_all[3:22], c, d)
+    w, c, d, sums = carries(1, x1, squares(r1))
+    w = corrected(w, left_all[3:], right_all[3:], c, d)
 
     u = to_wave(*padded(*w))
     n1 = [gather_taps(v, 16) + RIDGE * r for v, r in zip(u, r1)]
@@ -486,20 +519,23 @@
             pltpu.VMEM((2, 768, 256), BF16),
             pltpu.VMEM((GROUP, 16, 128), F32),
             pltpu.VMEM((GROUP, 8, 128), F32),
-            pltpu.VMEM((16, GROUP, 128), F32),
+            pltpu.VMEM((12, GROUP, 128), F32),
             pltpu.VMEM((8, GROUP, 128), F32),
-            pltpu.VMEM((2, 32, 8, 128), F32),
-            pltpu.VMEM((32, 8, 128), F32),
+            pltpu.VMEM((2, 22, 8, 128), F32),
+            pltpu.VMEM((24, 8, 128), F32),
             pltpu.VMEM((2, NX, 2, 8, 128), F32),
             pltpu.VMEM((2, NZ, 2, 8, 128), F32),
             pltpu.VMEM((2, NX, 40, 128), F32),
             pltpu.VMEM((2, NZ, 40, 128), F32),
             pltpu.VMEM((NX, 16, 128), F32),
             pltpu.VMEM((NZ, 16, 128), F32),
+            pltpu.VMEM((3, 2, 3, 8, 128), F32),
+            pltpu.VMEM((3, 2, 3, 8, 128), F32),
             dma((5,)),
             dma((2,)),
             dma, dma, dma, dma, dma, dma, dma, dma,
             dma((2,)), dma((2,)), dma((2,)), dma((2,)),
+            dma((3,)), dma((3,)),
         ],
         name="invert",
         compiler_params=pltpu.CompilerParams(

time: 41.7 us -> 38.9 us (0.933)
  Pallas kernels: 40.2 us -> 37.5 us
    pallas_call x1, Pallas kernels: 40.2 us -> 37.5 us  [body(): pl.pallas_call(kernel, out_shape=(out, out, out, jax.ShapeDtypeStruct((8,...]
where the time goes in v5:
time: 38.9 us; the launch traced here: 38.8 us
  Pallas kernels  37.5 us (96%)
  other arithmetic  0.73 us (2%)
  between operations  0.65 us (2%)
    pallas_call x1, Pallas kernels, body(): pl.pallas_call(kernel, out_shape=(out, out, out, jax.ShapeDtypeStruct((8,...  37.5 us

profile of v5, /device:TPU:8, one launch (start us, length us, event | category | flops | bytes accessed | tf_op | source)
XLA Modules:
  0.0 38.8 jit_solution(6118517926571037466)
XLA Ops:
  0.6 37.5 %invert.1 = (f32[2,16,1024]{2,1,0:T(8,128)S(1)}, f32[2,16,1024]{2,1,0:T(8,128)S(1)}, f32[2,16,1024]{2,1,0:T(8,128)S(1)}, f32[8,1024]{1,0:T(8,128)S(1)}) custom-call(f32[2,32,512]{2,1,0:T(8,128)} %obs_hbm.1, f32[4,1024]{1,0:T(4,128)} %win_hbm.1, f32[32,512]{1,0:T(8,128)} %dec_hbm.1, f32[2,256,256]{2,1,0:T(8,128)} %constant.4.clone.mats_hbm, ...), custom_call_target="tpu_custom_call" | custom-call | tf_op jit(solution)/shard_map/invert/pallas_call | solution.py:508
  38.1 0.7 %fusion = (f32[2,16,1024]{2,1,0:T(8,128)}, f32[2,16,1024]{2,1,0:T(8,128)}) fusion(f32[2,16,1024]{2,1,0:T(8,128)S(1)} %get-tuple-element.8, f32[2,16,1024]{2,1,0:T(8,128)S(1)} %get-tuple-element.9, f32[2,16,1024]{2,1,0:T(8,128)S(1)} %get-tuple-element.6, f32[1024]{0:T(1024)S(1)} %bitcast.1), kind=kLoop, calls=%fused_computation.1 | loop fusion | flops 98304 | bytes 659456 | tf_op jit(solution)/shard_map/sub | solution.py:545
  (1 shorter events, 0.0 us)

commit v6 on v5

--- a/solution.py
+++ b/solution.py
@@ -38,10 +38,10 @@
 def kernel(
     obs_hbm, win_hbm, dec_hbm, mats_hbm, tabs_hbm, base_ref, mid_ref, drop_ref, share_ref,
     obs_v, win_v, dec_v, full_v, tabs_v, mats_v, stage_o, stage_d, got_o, got_d,
-    spec, dec, carry_x, carry_z, xb, zb, cx, cz, out_halo, in_halo,
+    spec, dec, carry_x, xb, zb, cx, cz, out_halo, in_halo, in_dec,
     in_sem, own_sem, o_send, o_recv, d_send, d_recv, xc_send, xc_recv,
     zc_send, zc_recv, x_send, x_recv, z_send, z_recv,
-    h_send, h_recv,
+    h_send, h_recv, hd_send, hd_recv,
 ):
     me = lax.axis_index("chan")
     mz = me // NX
@@ -112,13 +112,13 @@
         [moved(white[0], -3), moved(white[1], -3), moved(white[0], 8), moved(white[1], 8)], axis=0
     )
     stage_o[...] = packed.T.reshape(GROUP, 16, 128)
-    packed = jnp.concatenate([moved(af, 6 * t - 3) for t in range(4)], axis=0)
+    packed = jnp.concatenate([moved(af, 4 * t) for t in range(4)], axis=0)
     stage_d[...] = packed.T.reshape(GROUP, 16, 128)[:, :8]
 
     pl.semaphore_wait(barrier, GROUP - 1)
 
     for stage, got, rows, send, recv in (
-        (stage_d, got_d, 6, d_send, d_recv), (stage_o, got_o, 11, o_send, o_recv)
+        (stage_d, got_d, 4, d_send, d_recv), (stage_o, got_o, 11, o_send, o_recv)
     ):
         for to in others:
             copy = pltpu.make_async_remote_copy(
@@ -128,7 +128,7 @@
             )
             copy.start()
     own = [
-        pltpu.make_async_copy(stage_d.at[me, pl.ds(0, 6)], got_d.at[pl.ds(0, 6), me, :], own_sem.at[0]),
+        pltpu.make_async_copy(stage_d.at[me, pl.ds(0, 4)], got_d.at[:, me, :], own_sem.at[0]),
         pltpu.make_async_copy(stage_o.at[me, pl.ds(0, 11)], got_o.at[pl.ds(0, 11), me, :], own_sem.at[1]),
     ]
     for copy in own:
@@ -214,7 +214,7 @@
         pltpu.make_async_copy(ref, ref, sem).wait()
 
     own[0].wait()
-    wait_for(got_d.at[pl.ds(0, 6), pl.ds(0, GROUP - 1)], d_recv)
+    wait_for(got_d.at[:, pl.ds(0, GROUP - 1)], d_recv)
 
     lane8 = lax.broadcasted_iota(jnp.int32, (8, 128), 1)
     low64 = lane8 < 64
@@ -231,13 +231,20 @@
             z[i + 1] = jnp.where(low32, pltpu.roll(y[i], 96, axis=1), y[i + 1])
         return z
 
-    for q in range(2):
-        turned = got_d[4 * q : 4 * q + 4].reshape(128, 128).T
-        for part in range(4):
-            base = part * 32
-            out = exchange([turned[base + 8 * i : base + 8 * i + 8] for i in range(4)])
-            for r in range(min(4, 6 - 4 * q)):
-                dec[6 * part + 4 * q + r] = out[r]
+    turned = got_d[...].reshape(128, 128).T
+    for part in range(4):
+        base = part * 32
+        out = exchange([turned[base + 8 * i : base + 8 * i + 8] for i in range(4)])
+        for r in range(4):
+            dec[3 + 4 * part + r] = out[r]
+
+    def send_to(src, dst, send, recv, to):
+        pltpu.make_async_remote_copy(
+            src_ref=src, dst_ref=dst, send_sem=send, recv_sem=recv, device_id={"chan": to}, device_id_type=MESH,
+        ).start()
+
+    after = lax.rem(me + 1, GROUP)
+    before = lax.rem(me + GROUP - 1, GROUP)
 
     def inverse(a):
         return jnp.where(a > 0.0, 1.0 / jnp.where(a > 0.0, a, 1.0), 0.0)
@@ -257,28 +264,54 @@
         for f in (20, 21):
             g[f] = (g[f - 1] - e[f - 1]) * inv[f]
 
-    inv = {f: inverse(dec[f]) for f in (1, 2, 19, 20, 21)}
-    twice = {f: 2.0 * (1.0 - dec[f]) for f in range(22)}
-    prods = {2: jnp.ones((8, 128), F32), 1: inv[2], 0: inv[1] * inv[2]}
-    for f in range(3, 22):
+    twice = {f: 2.0 * (1.0 - dec[f]) for f in range(3, 19)}
+    prods = {2: jnp.ones((8, 128), F32)}
+    for f in range(3, 19):
         prods[f] = dec[f] * prods[f - 1]
-    from_c = {f: 2.0 * prods[f] for f in range(22)}
+    from_c = {f: 2.0 * prods[f] for f in range(3, 19)}
     back_c = backward(from_c)
-    backward_left(from_c, back_c)
-    backward_right(from_c, back_c)
-    back_d = {18: jnp.ones((8, 128), F32), 19: inv[19]}
-    for f in range(17, -1, -1):
+    back_d = {18: jnp.ones((8, 128), F32)}
+    for f in range(17, 2, -1):
         back_d[f] = dec[f + 1] * back_d[f + 1]
-    for f in (20, 21):
-        back_d[f] = back_d[f - 1] * inv[f]
-    left_all = jnp.stack([from_c[f] + twice[f] * back_c[f] for f in range(22)])
-    right_all = jnp.stack([twice[f] * back_d[f] for f in range(22)])
+    left = {f: from_c[f] + twice[f] * back_c[f] for f in range(3, 19)}
+    right = {f: twice[f] * back_d[f] for f in range(3, 19)}
+    inv = {}
+
+    def halo_coefficients():
+        for side in range(2):
+            wait_for(in_dec.at[side], hd_recv.at[side])
+            wait_for(in_dec.at[side], hd_send.at[side])
+        for f in range(3):
+            dec[f] = jnp.where(me == 0, 0.0, in_dec[0, f])
+            dec[19 + f] = jnp.where(me == GROUP - 1, 0.0, in_dec[1, f])
+        halo = (0, 1, 2, 19, 20, 21)
+        for f in (1, 2, 19, 20, 21):
+            inv[f] = inverse(dec[f])
+        for f in halo:
+            twice[f] = 2.0 * (1.0 - dec[f])
+        prods[1] = inv[2]
+        prods[0] = inv[1] * inv[2]
+        for f in (19, 20, 21):
+            prods[f] = dec[f] * prods[f - 1]
+        for f in halo:
+            from_c[f] = 2.0 * prods[f]
+        backward_left(from_c, back_c)
+        backward_right(from_c, back_c)
+        for f in (2, 1, 0):
+            back_d[f] = dec[f + 1] * back_d[f + 1]
+        back_d[19] = inv[19]
+        for f in (20, 21):
+            back_d[f] = back_d[f - 1] * inv[f]
+        for f in halo:
+            left[f] = from_c[f] + twice[f] * back_c[f]
+            right[f] = twice[f] * back_d[f]
+
     cx[mx, 0:8] = prods[18]
     cx[mx, 8:16] = dec[3] * back_c[3]
 
     def x_copies(part, send, recv):
         out = []
-        for t in range(1, NX):
+        for t in (2, 1, 3):
             to = mz * NX + lax.rem(mx + t, NX)
             out.append(pltpu.make_async_remote_copy(
                 src_ref=part, dst_ref=part, send_sem=send, recv_sem=recv,
@@ -316,10 +349,7 @@
         for n in range(2):
             for f in range(3):
                 out_halo[slot, n, f] = x[n][first + f]
-        pltpu.make_async_remote_copy(
-            src_ref=out_halo.at[slot], dst_ref=in_halo.at[slot], send_sem=h_send.at[slot], recv_sem=h_recv.at[slot],
-            device_id={"chan": to}, device_id_type=MESH,
-        ).start()
+        send_to(out_halo.at[slot], in_halo.at[slot], h_send.at[slot], h_recv.at[slot], to)
 
     def halo_frames(slot, outside):
         wait_for(in_halo.at[slot], h_recv.at[slot])
@@ -328,14 +358,16 @@
             jnp.where(outside, 0.0, jnp.stack([in_halo[slot, 0, f], in_halo[slot, 1, f]])) for f in range(3)
         ]
 
-    def local_whiten(x):
+    def local_sums(x):
+        frames_x = {f: jnp.stack([x[0][f - 3], x[1][f - 3]]) for f in range(3, 19)}
+        going_right = 0.5 * sum(right[f] * frames_x[f] for f in range(3, 19))
+        going_left = 0.5 * sum(left[f] * frames_x[f] for f in range(3, 19))
         s = {2: jnp.zeros((2, 8, 128), F32)}
         e = {}
         for f in range(3, 19):
-            own_x = jnp.stack([x[0][f - 3], x[1][f - 3]])
-            s[f] = dec[f] * s[f - 1] + (1.0 - dec[f]) * own_x
-            e[f] = own_x + 2.0 * s[f]
-        return s, e, backward(e)
+            s[f] = dec[f] * s[f - 1] + (1.0 - dec[f]) * frames_x[f]
+            e[f] = frames_x[f] + 2.0 * s[f]
+        return going_right, going_left, s, e
 
     def left_whiten(x, s, e, g):
         for f in (2, 1, 0):
@@ -395,70 +427,114 @@
         cz[mz, 8:16] = gk
         z_copies(cz.at[mz], zc_send, zc_recv)
 
+    def own_of(ref, values, index):
+        for n, value in enumerate(values):
+            ref[n] = value
+        return ref[index]
+
+    def ahead_weights(a, k):
+        one = jnp.ones((8, 128), F32)
+        none = jnp.zeros((8, 128), F32)
+        wc, wh, wd = [none] * NZ, [none] * NZ, [none] * NZ
+        run = one
+        for n in range(NZ - 1, -1, -1):
+            wc[n] = jnp.where(n < mz, run, none)
+            run = jnp.where(n < mz, run * a[n], run)
+        run = one
+        for n in range(NZ):
+            wh[n] = jnp.where(n > mz, run, none)
+            run = jnp.where(n > mz, run * a[n], run)
+        through = none
+        of_c = none
+        for n in range(NZ - 1, -1, -1):
+            if n < NZ - 1:
+                through = wh[n + 1] * k[n + 1] + a[n + 1] * through
+            wd[n] = jnp.where(n < mz, none, through)
+            of_c = jnp.where(n == mz, a[n] * through, of_c)
+        for n in range(NZ):
+            wd[n] = wd[n] + of_c * wc[n]
+        return wc, wh, wd
+
+    saved = {}
+
     def carries(turn, x, row):
-        s, e, g = local_whiten(x)
+        going_right, going_left, s, e = local_sums(x)
         xv = xb.at[turn, mx]
-        write_pair(xv, 0, s[18])
-        write_pair(xv, 16, dec[3] * g[3])
+        write_pair(xv, 0, going_right)
+        write_pair(xv, 16, going_left)
         square = sum(e[f] * e[f] for f in range(3, 19))
         xv[32:33] = row_sum(square[0] + square[1])
         xv[33:34] = row
         x_copies(xb.at[turn, mx, pl.ds(0, 34)], x_send.at[turn], x_recv.at[turn])
         if turn == 0:
-            halo_copy(0, x, 13, lax.rem(me + 1, GROUP))
-            halo_copy(1, x, 0, lax.rem(me + GROUP - 1, GROUP))
+            halo_copy(0, x, 13, after)
+            halo_copy(1, x, 0, before)
+            send_to(dec.at[pl.ds(16, 3)], in_dec.at[0], hd_send.at[0], hd_recv.at[0], after)
+            send_to(dec.at[pl.ds(3, 3)], in_dec.at[1], hd_send.at[1], hd_recv.at[1], before)
             group_coefficients()
         else:
-            halo_copy(2, x, 0, lax.rem(me + GROUP - 1, GROUP))
+            halo_copy(2, x, 0, before)
+        g = backward(e)
         a, k = [[cx[n, 8 * m : 8 * m + 8] for n in range(NX)] for m in range(2)]
         if turn == 0:
-            wait_for(stage_d.at[pl.ds(0, GROUP - 1), pl.ds(0, 6)], d_send)
+            wait_for(stage_d.at[pl.ds(0, GROUP - 1), pl.ds(0, 4)], d_send)
             wait_for(stage_o.at[pl.ds(0, GROUP - 1), pl.ds(0, 11)], o_send)
             wait_for(cx.at[pl.ds(0, NX - 1)], xc_send)
         else:
             wait_for(cz.at[pl.ds(0, NZ - 1)], zc_send)
             wait_for(zb.at[0, pl.ds(0, NZ - 1), pl.ds(0, 34)], z_send.at[0])
         wait_for(xb.at[turn, pl.ds(0, NX - 1), pl.ds(0, 34)], x_recv.at[turn])
-        left = [pair(xb.at[turn, n], 0) for n in range(NX)]
-        right = [pair(xb.at[turn, n], 16) for n in range(NX)]
-        cs, _, out = chain(zero, zero, left, right, a, k)
+        lefts = [pair(xb.at[turn, n], 0) for n in range(NX)]
+        rights = [pair(xb.at[turn, n], 16) for n in range(NX)]
+        cs, ds, out = chain(zero, zero, lefts, rights, a, k)
         zv = zb.at[turn, mz]
         write_pair(zv, 0, cs[NX])
         write_pair(zv, 16, out)
-        zv[32:33] = crossed(cs[:NX], right, k) + sum(xb[turn, n, 32:33] for n in range(NX))
+        zv[32:33] = crossed(cs[:NX], rights, k) + sum(xb[turn, n, 32:33] for n in range(NX))
         zv[33:34] = sum(xb[turn, n, 33:34] for n in range(NX))
         z_copies(zb.at[turn, mz, pl.ds(0, 34)], z_send.at[turn], z_recv.at[turn])
+        c_own = own_of(carry_x.at[0], cs[:NX], mx)
+        d_own = own_of(carry_x.at[1], ds, mx)
         if turn == 0:
+            one = jnp.ones((2, 8, 128), F32)
+            quiet = [zero] * NX
+            from_left, back_left, _ = chain(one, zero, quiet, quiet, a, k)
+            _, back_right, _ = chain(zero, one, quiet, quiet, a, k)
+            pass_c = own_of(carry_x.at[2], from_left[:NX], mx)[0]
+            turn_c = own_of(carry_x.at[3], back_left, mx)[0]
+            pass_d = own_of(carry_x.at[4], back_right, mx)[0]
+            halo_coefficients()
             left_whiten(halo_frames(0, me == 0), s, e, g)
+            wait_for(cz.at[pl.ds(0, NZ - 1)], zc_recv)
+            za, zk = [[cz[n, 8 * m : 8 * m + 8] for n in range(NZ)] for m in range(2)]
+            wc, wh, wd = ahead_weights(za, zk)
+            saved["z"] = za, zk
+            saved["c"] = [pass_c * w for w in wc]
+            saved["h"] = [pass_d * w for w in wh]
+            saved["l"] = [pass_d * v + turn_c * w for v, w in zip(wd, wc)]
+        za, zk = saved["z"]
         right_whiten(halo_frames(1 + turn, me == GROUP - 1), s, e, g)
         w = whole(e, g, 3 * turn)
-        if turn == 0:
-            wait_for(cz.at[pl.ds(0, NZ - 1)], zc_recv)
-        za, zk = [[cz[n, 8 * m : 8 * m + 8] for n in range(NZ)] for m in range(2)]
         wait_for(xb.at[turn, pl.ds(0, NX - 1), pl.ds(0, 34)], x_send.at[turn])
         wait_for(zb.at[turn, pl.ds(0, NZ - 1), pl.ds(0, 34)], z_recv.at[turn])
         zleft = [pair(zb.at[turn, n], 0) for n in range(NZ)]
         zright = [pair(zb.at[turn, n], 16) for n in range(NZ)]
-        zcs, zds, _ = chain(zero, zero, zleft, zright, za, zk)
-        for n in range(NZ):
-            carry_z[0, n] = zcs[n]
-            carry_z[1, n] = zds[n]
-        cs, ds, _ = chain(carry_z[0, mz], carry_z[1, mz], left, right, a, k)
-        for n in range(NX):
-            carry_x[0, n] = cs[n]
-            carry_x[1, n] = ds[n]
+        c = c_own + sum(v * z for v, z in zip(saved["c"], zleft))
+        d = d_own + sum(v * z for v, z in zip(saved["h"], zright)) + sum(v * z for v, z in zip(saved["l"], zleft))
 
         def sums():
-            squares = crossed(zcs[:NZ], zright, zk) + sum(zb[turn, n, 32:33] for n in range(NZ))
+            zcs = [zero]
+            for n in range(NZ - 1):
+                zcs.append(za[n] * zcs[n] + zleft[n])
+            squares = crossed(zcs, zright, zk) + sum(zb[turn, n, 32:33] for n in range(NZ))
             rows = sum(zb[turn, n, 33:34] for n in range(NZ))
             return jnp.sum(squares, axis=1, keepdims=True), jnp.sum(rows, axis=1, keepdims=True)
 
-        return w, carry_x[0, mx], carry_x[1, mx], sums
-
-    def corrected(w, left, right, c, d):
-        re = jnp.stack([v[0] for v in w]) + left * c[0] + right * d[0]
-        im = jnp.stack([v[1] for v in w]) + left * c[1] + right * d[1]
-        return re, im
+        return w, c, d, sums
+
+    def corrected(w, start, c, d):
+        out = [v + left[f] * c + right[f] * d for f, v in zip(range(start, 22), w)]
+        return jnp.stack([v[0] for v in out]), jnp.stack([v[1] for v in out])
 
     def padded(re, im):
         fill = jnp.zeros((1, 8, 128), F32)
@@ -472,7 +548,7 @@
     x0 = to_spec(*[spread_taps(v, 16) for v in r0])
     mine_r0 = [v[3:] for v in r0]
     w, c, d, sums = carries(0, x0, squares(mine_r0))
-    w = corrected(w, left_all, right_all, c, d)
+    w = corrected(w, 0, c, d)
 
     u = to_wave(*w)
     q1 = [part_only(gather_taps(v, 19) + RIDGE * r) for v, r in zip(u, r0)]
@@ -483,7 +559,7 @@
     mine_q1 = [v[3:] for v in q1]
     r1 = [r - alpha * q for r, q in zip(mine_r0, mine_q1)]
     w, c, d, sums = carries(1, x1, squares(r1))
-    w = corrected(w, left_all[3:], right_all[3:], c, d)
+    w = corrected(w, 3, c, d)
 
     u = to_wave(*padded(*w))
     n1 = [gather_taps(v, 16) + RIDGE * r for v, r in zip(u, r1)]
@@ -520,22 +596,23 @@
             pltpu.VMEM((GROUP, 16, 128), F32),
             pltpu.VMEM((GROUP, 8, 128), F32),
             pltpu.VMEM((12, GROUP, 128), F32),
-            pltpu.VMEM((8, GROUP, 128), F32),
+            pltpu.VMEM((4, GROUP, 128), F32),
             pltpu.VMEM((2, 22, 8, 128), F32),
             pltpu.VMEM((24, 8, 128), F32),
-            pltpu.VMEM((2, NX, 2, 8, 128), F32),
-            pltpu.VMEM((2, NZ, 2, 8, 128), F32),
+            pltpu.VMEM((5, NX, 2, 8, 128), F32),
             pltpu.VMEM((2, NX, 40, 128), F32),
             pltpu.VMEM((2, NZ, 40, 128), F32),
             pltpu.VMEM((NX, 16, 128), F32),
             pltpu.VMEM((NZ, 16, 128), F32),
             pltpu.VMEM((3, 2, 3, 8, 128), F32),
             pltpu.VMEM((3, 2, 3, 8, 128), F32),
+            pltpu.VMEM((2, 3, 8, 128), F32),
             dma((5,)),
             dma((2,)),
             dma, dma, dma, dma, dma, dma, dma, dma,
             dma((2,)), dma((2,)), dma((2,)), dma((2,)),
             dma((3,)), dma((3,)),
+            dma((2,)), dma((2,)),
         ],
         name="invert",
         compiler_params=pltpu.CompilerParams(

time: 38.9 us -> 38.1 us (0.979)
  Pallas kernels: 37.5 us -> 36.7 us
    pallas_call x1, Pallas kernels: 37.5 us -> 36.7 us  [body(): pl.pallas_call(kernel, out_shape=(out, out, out, jax.ShapeDtypeStruct((8,...]
where the time goes in v6:
time: 38.1 us; the launch traced here: 38 us
  Pallas kernels  36.7 us (96%)
  other arithmetic  0.73 us (2%)
  between operations  0.65 us (2%)
    pallas_call x1, Pallas kernels, body(): pl.pallas_call(kernel, out_shape=(out, out, out, jax.ShapeDtypeStruct((8,...  36.7 us

profile of v6, /device:TPU:8, one launch (start us, length us, event | category | flops | bytes accessed | tf_op | source)
XLA Modules:
  0.0 38.0 jit_solution(8967321200829618995)
XLA Ops:
  0.6 36.7 %invert.1 = (f32[2,16,1024]{2,1,0:T(8,128)S(1)}, f32[2,16,1024]{2,1,0:T(8,128)S(1)}, f32[2,16,1024]{2,1,0:T(8,128)S(1)}, f32[8,1024]{1,0:T(8,128)S(1)}) custom-call(f32[2,32,512]{2,1,0:T(8,128)} %obs_hbm.1, f32[4,1024]{1,0:T(4,128)} %win_hbm.1, f32[32,512]{1,0:T(8,128)} %dec_hbm.1, f32[2,256,256]{2,1,0:T(8,128)} %constant.4.clone.mats_hbm, ...), custom_call_target="tpu_custom_call" | custom-call | tf_op jit(solution)/shard_map/invert/pallas_call | solution.py:584
  37.3 0.7 %fusion = (f32[2,16,1024]{2,1,0:T(8,128)}, f32[2,16,1024]{2,1,0:T(8,128)}) fusion(f32[2,16,1024]{2,1,0:T(8,128)S(1)} %get-tuple-element.8, f32[2,16,1024]{2,1,0:T(8,128)S(1)} %get-tuple-element.9, f32[2,16,1024]{2,1,0:T(8,128)S(1)} %get-tuple-element.6, f32[1024]{0:T(1024)S(1)} %bitcast.1), kind=kLoop, calls=%fused_computation.1 | loop fusion | flops 98304 | bytes 659456 | tf_op jit(solution)/shard_map/sub | solution.py:622
  (1 shorter events, 0.0 us)

commit v7 on v6

--- a/solution.py
+++ b/solution.py
@@ -38,10 +38,10 @@
 def kernel(
     obs_hbm, win_hbm, dec_hbm, mats_hbm, tabs_hbm, base_ref, mid_ref, drop_ref, share_ref,
     obs_v, win_v, dec_v, full_v, tabs_v, mats_v, stage_o, stage_d, got_o, got_d,
-    spec, dec, carry_x, xb, zb, cx, cz, out_halo, in_halo, in_dec,
+    spec, dec, carry_x, xb, zb, cx, cz, out_halo, in_halo,
     in_sem, own_sem, o_send, o_recv, d_send, d_recv, xc_send, xc_recv,
     zc_send, zc_recv, x_send, x_recv, z_send, z_recv,
-    h_send, h_recv, hd_send, hd_recv,
+    h_send, h_recv,
 ):
     me = lax.axis_index("chan")
     mz = me // NX
@@ -51,9 +51,6 @@
         ((dz, dx) for dz in range(NZ) for dx in range(NX) if dz or dx),
         key=lambda o: -min(o[0], NZ - o[0]) - min(o[1], NX - o[1]),
     )
-    others = [lax.rem(mz + dz, NZ) * NX + lax.rem(mx + dx, NX) for dz, dx in others]
-    for to in others:
-        pl.semaphore_signal(barrier, inc=1, device_id={"chan": to}, device_id_type=MESH)
     inputs = []
     for t, (src, dst) in enumerate(
         ((obs_hbm, obs_v), (dec_hbm, dec_v), (win_hbm, win_v), (mats_hbm, full_v), (tabs_hbm, tabs_v))
@@ -61,6 +58,9 @@
         copy = pltpu.make_async_copy(src, dst, in_sem.at[t])
         copy.start()
         inputs.append(copy)
+    others = [lax.rem(mz + dz, NZ) * NX + lax.rem(mx + dx, NX) for dz, dx in others]
+    for to in others:
+        pl.semaphore_signal(barrier, inc=1, device_id={"chan": to}, device_id_type=MESH)
     inputs[0].wait()
     inputs[1].wait()
 
@@ -115,6 +115,13 @@
     packed = jnp.concatenate([moved(af, 4 * t) for t in range(4)], axis=0)
     stage_d[...] = packed.T.reshape(GROUP, 16, 128)[:, :8]
 
+    own = [
+        pltpu.make_async_copy(stage_d.at[me, pl.ds(0, 4)], got_d.at[:, me, :], own_sem.at[0]),
+        pltpu.make_async_copy(stage_o.at[me, pl.ds(0, 11)], got_o.at[pl.ds(0, 11), me, :], own_sem.at[1]),
+    ]
+    for copy in own:
+        copy.start()
+
     pl.semaphore_wait(barrier, GROUP - 1)
 
     for stage, got, rows, send, recv in (
@@ -127,12 +134,6 @@
                 device_id={"chan": to}, device_id_type=MESH,
             )
             copy.start()
-    own = [
-        pltpu.make_async_copy(stage_d.at[me, pl.ds(0, 4)], got_d.at[:, me, :], own_sem.at[0]),
-        pltpu.make_async_copy(stage_o.at[me, pl.ds(0, 11)], got_o.at[pl.ds(0, 11), me, :], own_sem.at[1]),
-    ]
-    for copy in own:
-        copy.start()
     for copy in inputs[2:]:
         copy.wait()
 
@@ -270,20 +271,12 @@
         prods[f] = dec[f] * prods[f - 1]
     from_c = {f: 2.0 * prods[f] for f in range(3, 19)}
     back_c = backward(from_c)
-    back_d = {18: jnp.ones((8, 128), F32)}
-    for f in range(17, 2, -1):
-        back_d[f] = dec[f + 1] * back_d[f + 1]
-    left = {f: from_c[f] + twice[f] * back_c[f] for f in range(3, 19)}
-    right = {f: twice[f] * back_d[f] for f in range(3, 19)}
-    inv = {}
+    back_d, left, right, inv = {18: jnp.ones((8, 128), F32)}, {}, {}, {}
 
     def halo_coefficients():
-        for side in range(2):
-            wait_for(in_dec.at[side], hd_recv.at[side])
-            wait_for(in_dec.at[side], hd_send.at[side])
         for f in range(3):
-            dec[f] = jnp.where(me == 0, 0.0, in_dec[0, f])
-            dec[19 + f] = jnp.where(me == GROUP - 1, 0.0, in_dec[1, f])
+            dec[f] = jnp.where(me == 0, 0.0, in_halo[0, 2, f])
+            dec[19 + f] = jnp.where(me == GROUP - 1, 0.0, in_halo[1, 2, f])
         halo = (0, 1, 2, 19, 20, 21)
         for f in (1, 2, 19, 20, 21):
             inv[f] = inverse(dec[f])
@@ -336,6 +329,12 @@
     own[1].wait()
     wait_for(got_o.at[pl.ds(0, 11), pl.ds(0, GROUP - 1)], o_recv)
 
+    for f in range(17, 2, -1):
+        back_d[f] = dec[f + 1] * back_d[f + 1]
+    for f in range(3, 19):
+        left[f] = from_c[f] + twice[f] * back_c[f]
+        right[f] = twice[f] * back_d[f]
+
     for q in range(3):
         turned = got_o[4 * q : 4 * q + 4].reshape(128, 128).T
         for half in range(2):
@@ -346,14 +345,21 @@
                     spec[c, 11 * half + 4 * q + r] = out[r]
 
     def halo_copy(slot, x, first, to):
-        for n in range(2):
-            for f in range(3):
-                out_halo[slot, n, f] = x[n][first + f]
-        send_to(out_halo.at[slot], in_halo.at[slot], h_send.at[slot], h_recv.at[slot], to)
+        planes = 3 if slot < 2 else 2
+        for f in range(3):
+            out_halo[slot, 0, f] = x[0][first + f]
+            out_halo[slot, 1, f] = x[1][first + f]
+            if planes == 3:
+                out_halo[slot, 2, f] = dec[3 + first + f]
+        part = (slot, pl.ds(0, planes))
+        send_to(out_halo.at[part], in_halo.at[part], h_send.at[slot], h_recv.at[slot], to)
+
+    def halo_wait(slot):
+        part = (slot, pl.ds(0, 3 if slot < 2 else 2))
+        wait_for(in_halo.at[part], h_recv.at[slot])
+        wait_for(out_halo.at[part], h_send.at[slot])
 
     def halo_frames(slot, outside):
-        wait_for(in_halo.at[slot], h_recv.at[slot])
-        wait_for(out_halo.at[slot], h_send.at[slot])
         return [
             jnp.where(outside, 0.0, jnp.stack([in_halo[slot, 0, f], in_halo[slot, 1, f]])) for f in range(3)
         ]
@@ -455,6 +461,17 @@
             wd[n] = wd[n] + of_c * wc[n]
         return wc, wh, wd
 
+    def group_weights(a, k):
+        one = jnp.ones((8, 128), F32)
+        gl, gh = [one], [one]
+        for n in range(NX - 1):
+            gl.insert(0, gl[0] * a[NX - 1 - n])
+            gh.append(gh[n] * a[n])
+        gm = [gh[NX - 1] * k[NX - 1]]
+        for n in range(NX - 2, 0, -1):
+            gm.insert(0, gh[n] * k[n] + a[n] * gm[0])
+        return gl, gh, gm
+
     saved = {}
 
     def carries(turn, x, row):
@@ -469,8 +486,6 @@
         if turn == 0:
             halo_copy(0, x, 13, after)
             halo_copy(1, x, 0, before)
-            send_to(dec.at[pl.ds(16, 3)], in_dec.at[0], hd_send.at[0], hd_recv.at[0], after)
-            send_to(dec.at[pl.ds(3, 3)], in_dec.at[1], hd_send.at[1], hd_recv.at[1], before)
             group_coefficients()
         else:
             halo_copy(2, x, 0, before)
@@ -486,10 +501,11 @@
         wait_for(xb.at[turn, pl.ds(0, NX - 1), pl.ds(0, 34)], x_recv.at[turn])
         lefts = [pair(xb.at[turn, n], 0) for n in range(NX)]
         rights = [pair(xb.at[turn, n], 16) for n in range(NX)]
-        cs, ds, out = chain(zero, zero, lefts, rights, a, k)
+        cs, ds, _ = chain(zero, zero, lefts, rights, a, k)
+        gl, gh, gm = group_weights(a, k)
         zv = zb.at[turn, mz]
-        write_pair(zv, 0, cs[NX])
-        write_pair(zv, 16, out)
+        write_pair(zv, 0, sum(v * z for v, z in zip(gl, lefts)))
+        write_pair(zv, 16, sum(v * z for v, z in zip(gh, rights)) + sum(v * z for v, z in zip(gm, lefts[:-1])))
         zv[32:33] = crossed(cs[:NX], rights, k) + sum(xb[turn, n, 32:33] for n in range(NX))
         zv[33:34] = sum(xb[turn, n, 33:34] for n in range(NX))
         z_copies(zb.at[turn, mz, pl.ds(0, 34)], z_send.at[turn], z_recv.at[turn])
@@ -503,6 +519,8 @@
             pass_c = own_of(carry_x.at[2], from_left[:NX], mx)[0]
             turn_c = own_of(carry_x.at[3], back_left, mx)[0]
             pass_d = own_of(carry_x.at[4], back_right, mx)[0]
+            halo_wait(0)
+            halo_wait(1)
             halo_coefficients()
             left_whiten(halo_frames(0, me == 0), s, e, g)
             wait_for(cz.at[pl.ds(0, NZ - 1)], zc_recv)
@@ -512,6 +530,8 @@
             saved["c"] = [pass_c * w for w in wc]
             saved["h"] = [pass_d * w for w in wh]
             saved["l"] = [pass_d * v + turn_c * w for v, w in zip(wd, wc)]
+        if turn == 1:
+            halo_wait(2)
         za, zk = saved["z"]
         right_whiten(halo_frames(1 + turn, me == GROUP - 1), s, e, g)
         w = whole(e, g, 3 * turn)
@@ -604,15 +624,13 @@
             pltpu.VMEM((2, NZ, 40, 128), F32),
             pltpu.VMEM((NX, 16, 128), F32),
             pltpu.VMEM((NZ, 16, 128), F32),
-            pltpu.VMEM((3, 2, 3, 8, 128), F32),
-            pltpu.VMEM((3, 2, 3, 8, 128), F32),
-            pltpu.VMEM((2, 3, 8, 128), F32),
+            pltpu.VMEM((3, 3, 3, 8, 128), F32),
+            pltpu.VMEM((3, 3, 3, 8, 128), F32),
             dma((5,)),
             dma((2,)),
             dma, dma, dma, dma, dma, dma, dma, dma,
             dma((2,)), dma((2,)), dma((2,)), dma((2,)),
             dma((3,)), dma((3,)),
-            dma((2,)), dma((2,)),
         ],
         name="invert",
         compiler_params=pltpu.CompilerParams(

time: 38.1 us -> 38 us (level)
  no operation moved by 1% of the time
where the time goes in v7:
time: 38 us; the launch traced here: 37.9 us
  Pallas kernels  36.6 us (96%)
  other arithmetic  0.73 us (2%)
  between operations  0.65 us (2%)
    pallas_call x1, Pallas kernels, body(): pl.pallas_call(kernel, out_shape=(out, out, out, jax.ShapeDtypeStruct((8,...  36.6 us

profile of v7, /device:TPU:8, one launch (start us, length us, event | category | flops | bytes accessed | tf_op | source)
XLA Modules:
  0.0 37.9 jit_solution(11099954951772111247)
XLA Ops:
  0.6 36.6 %invert.1 = (f32[2,16,1024]{2,1,0:T(8,128)S(1)}, f32[2,16,1024]{2,1,0:T(8,128)S(1)}, f32[2,16,1024]{2,1,0:T(8,128)S(1)}, f32[8,1024]{1,0:T(8,128)S(1)}) custom-call(f32[2,32,512]{2,1,0:T(8,128)} %obs_hbm.1, f32[4,1024]{1,0:T(4,128)} %win_hbm.1, f32[32,512]{1,0:T(8,128)} %dec_hbm.1, f32[2,256,256]{2,1,0:T(8,128)} %constant.4.clone.mats_hbm, ...), custom_call_target="tpu_custom_call" | custom-call | tf_op jit(solution)/shard_map/invert/pallas_call | solution.py:604
  37.2 0.7 %fusion = (f32[2,16,1024]{2,1,0:T(8,128)}, f32[2,16,1024]{2,1,0:T(8,128)}) fusion(f32[2,16,1024]{2,1,0:T(8,128)S(1)} %get-tuple-element.8, f32[2,16,1024]{2,1,0:T(8,128)S(1)} %get-tuple-element.9, f32[2,16,1024]{2,1,0:T(8,128)S(1)} %get-tuple-element.6, f32[1024]{0:T(1024)S(1)} %bitcast.1), kind=kLoop, calls=%fused_computation.1 | loop fusion | flops 98304 | bytes 659456 | tf_op jit(solution)/shard_map/sub | solution.py:640
  (1 shorter events, 0.0 us)

commit v8 on v7

--- a/solution.py
+++ b/solution.py
@@ -127,7 +127,7 @@
     for stage, got, rows, send, recv in (
         (stage_d, got_d, 4, d_send, d_recv), (stage_o, got_o, 11, o_send, o_recv)
     ):
-        for to in others:
+        for to in (others[::-1] if rows < 11 else others):
             copy = pltpu.make_async_remote_copy(
                 src_ref=stage.at[to, pl.ds(0, rows)], dst_ref=got.at[pl.ds(0, rows), me, :],
                 send_sem=send, recv_sem=recv,

time: 38 us -> 38 us (level)
  no operation moved by 1% of the time
where the time goes in v8:
time: 38 us; the launch traced here: 37.9 us
  Pallas kernels  36.5 us (96%)
  other arithmetic  0.73 us (2%)
  between operations  0.65 us (2%)
    pallas_call x1, Pallas kernels, body(): pl.pallas_call(kernel, out_shape=(out, out, out, jax.ShapeDtypeStruct((8,...  36.5 us

profile of v8, /device:TPU:8, one launch (start us, length us, event | category | flops | bytes accessed | tf_op | source)
XLA Modules:
  0.0 37.9 jit_solution(8140578409993729590)
XLA Ops:
  0.6 36.5 %invert.1 = (f32[2,16,1024]{2,1,0:T(8,128)S(1)}, f32[2,16,1024]{2,1,0:T(8,128)S(1)}, f32[2,16,1024]{2,1,0:T(8,128)S(1)}, f32[8,1024]{1,0:T(8,128)S(1)}) custom-call(f32[2,32,512]{2,1,0:T(8,128)} %obs_hbm.1, f32[4,1024]{1,0:T(4,128)} %win_hbm.1, f32[32,512]{1,0:T(8,128)} %dec_hbm.1, f32[2,256,256]{2,1,0:T(8,128)} %constant.4.clone.mats_hbm, ...), custom_call_target="tpu_custom_call" | custom-call | tf_op jit(solution)/shard_map/invert/pallas_call | solution.py:604
  37.1 0.7 %fusion = (f32[2,16,1024]{2,1,0:T(8,128)}, f32[2,16,1024]{2,1,0:T(8,128)}) fusion(f32[2,16,1024]{2,1,0:T(8,128)S(1)} %get-tuple-element.8, f32[2,16,1024]{2,1,0:T(8,128)S(1)} %get-tuple-element.9, f32[2,16,1024]{2,1,0:T(8,128)S(1)} %get-tuple-element.6, f32[1024]{0:T(1024)S(1)} %bitcast.1), kind=kLoop, calls=%fused_computation.1 | loop fusion | flops 98304 | bytes 659456 | tf_op jit(solution)/shard_map/sub | solution.py:640
  (1 shorter events, 0.0 us)
